TPU v7x, 256 devices: a whole 4x4x8 slice. The times are simulated.
256 devices in a mesh: cell: 32 (over x, z), samp: 8 (over y, core).
Axes of the slice: x: 4, y: 4, z: 8, core: 2. Of those that a mesh axis runs over, the one named last changes fastest.
Arguments:
- bases: float32 [16, 65536, 192], P('samp', 'cell'), may hold values from -12 to 12
- reference_basis: float32 [65536, 192], P(('cell', 'samp')), may hold values from -5 to 5
- mass: float32 [65536], P('cell'), may hold values from 0.25 to 2.5
- interp_weights: float32 [16], P('samp'), may hold values from 0.2 to 1
Outputs:
- tangent: float32 [65536, 192], P(('cell', 'samp'))
All inputs are finite; a program needn't handle non-finite values.
Results may differ from a plain program's by a relative error of at most 0.0003.
Values sent between devices are 32-bit elements; how exact they have to be, the bound alone decides.
A program may use at most 64 MiB of HBM per device.

v0:
```python
import jax
import jax.numpy as jnp
from jax import lax
from jax.sharding import PartitionSpec as P

NTERMS = 6


HIGHEST_PRECISION = lax.Precision.HIGHEST


def invert(matrix):
    normal_matrix = jnp.matmul(matrix.T, matrix, precision=HIGHEST_PRECISION)
    factor = jnp.linalg.cholesky(normal_matrix)
    return jax.scipy.linalg.cho_solve((factor, True), matrix.T)


def series(curvature_gram):
    identity = jnp.eye(curvature_gram.shape[-1], dtype=curvature_gram.dtype)
    leading = (-1.0) ** (NTERMS - 1) / (2 * NTERMS - 1)
    result = jnp.broadcast_to(identity * leading, curvature_gram.shape)
    for degree in range(NTERMS - 2, -1, -1):
        result = identity * ((-1.0) ** degree / (2 * degree + 1)) + jnp.matmul(
            curvature_gram, result, precision=HIGHEST_PRECISION
        )
    return result


def body(bases, reference_basis, mass, interp_weights):
    whole_rows = bases.shape[1] * lax.axis_size("cell")
    inverse_rows = 1.0 / whole_rows
    panel_rows = lax.all_gather(reference_basis, "samp", axis=0, tiled=True)
    weighted = panel_rows * mass[:, None]
    cross_gram = (
        jnp.einsum("nr,knq->krq", weighted, bases, precision=HIGHEST_PRECISION) * inverse_rows
    )
    cross_gram = lax.psum(cross_gram, "cell")
    inverses = jax.vmap(invert)(cross_gram)
    shifted = (
        jnp.einsum("knr,krq->knq", bases, inverses, precision=HIGHEST_PRECISION) - panel_rows[None]
    )
    curvature_gram = (
        jnp.einsum(
            "knr,knq->krq", shifted * mass[None, :, None], shifted, precision=HIGHEST_PRECISION
        )
        * inverse_rows
    )
    curvature_gram = lax.psum(curvature_gram, "cell")
    factors = series(curvature_gram) * interp_weights[:, None, None]
    own_rows = bases.shape[1] // lax.axis_size("samp")
    complete = jnp.einsum("knr,krq->nq", shifted, factors, precision=HIGHEST_PRECISION)
    summed = lax.psum(complete, "samp")
    return lax.dynamic_slice_in_dim(summed, lax.axis_index("samp") * own_rows, own_rows, 0)


def solution(mesh):
    placed = (P("samp", "cell", None), P(("cell", "samp"), None), P("cell"), P("samp"))
    return jax.shard_map(
        body, mesh=mesh, in_specs=placed, out_specs=P(("cell", "samp"), None), check_vma=False
    )
```

profile of v0, /device:TPU:8, one launch (start us, length us, event | category | flops | bytes accessed | tf_op | source)
XLA Modules:
  0.0 554.5 jit_solution(13389752260291910251)
XLA Ops:
  11.0 26.6 %all-gather.2.cloned.1.call-done = f32[2048,192]{0,1:T(8,128)} async-done(((f32[256,192]{0,1:T(8,128)}), f32[2048,192]{0,1:T(8,128)}) %all-gather.2.cloned.1.call-update) | async-done | bytes 1572880 | tf_op jit(solution)/shard_map/all_gather | solution.py:32
  37.5 5.0 fusion.9
  44.1 145.6 %all-reduce.7.cloned.1.call-done = f32[2,192,192]{2,1,0:T(8,128)} async-done(((f32[2,192,192]{2,1,0:T(8,128)}), f32[2,192,192]{2,1,0:T(8,128)}) %all-reduce.7.cloned.1.call-update) | async-done | bytes 294928 | tf_op jit(solution)/shard_map/psum | solution.py:37
  189.7 2.8 fusion.40
  192.6 2.0 copy.17
  194.6 1.2 fusion.20
  197.1 24.9 %custom-call.20 = f32[2,128,128]{2,1,0:T(8,128)} custom-call(f32[2,128,128]{2,1,0:T(8,128)} %cholesky.129), custom_call_target="Cholesky" | custom-call | tf_op jit(solution)/shard_map/vmap(jit(cholesky))/cholesky | solution.py:14
  222.0 2.1 select_reduce_fusion
  224.2 21.1 %custom-call.21 = f32[2,1,128,128]{2,3,1,0:T(8,128)} custom-call(f32[2,1,128,128]{3,2,1,0:T(8,128)} %get-tuple-element.26), custom_call_target="InvertDiagBlocksLowerTriangular" | custom-call | tf_op jit(solution)/shard_map/vmap(jit(cholesky))/cholesky | solution.py:14
  245.3 1.7 cholesky.124
  246.9 1.8 constant_dynamic-update-slice_fusion.1
  248.8 1.7 convolution_subtract_fusion.2
  250.5 13.1 %custom-call.22 = f32[2,64,64]{2,1,0:T(8,128)} custom-call(f32[2,64,64]{2,1,0:T(8,128)} %convolution_subtract_fusion.2), custom_call_target="Cholesky" | custom-call | tf_op jit(solution)/shard_map/vmap(jit(cholesky))/cholesky | solution.py:14
  263.5 1.5 select_reduce_fusion.1
  269.5 40.8 %custom-call.23 = f32[2,2,128,128]{2,3,1,0:T(8,128)} custom-call(f32[2,2,128,128]{3,2,1,0:T(8,128)} %pad_maximum_fusion), custom_call_target="InvertDiagBlocksLowerTriangular" | custom-call | tf_op jit(solution)/shard_map/vmap(jit(_cho_solve))/triangular_solve | solution.py:15
  310.2 1.2 fusion.21
  311.5 1.2 convolution_subtract_fusion.1
  312.6 1.4 fusion.36
  315.1 1.3 convolution_subtract_fusion
  317.2 1.3 fusion.33
  318.5 4.4 bitcast_subtract_fusion
  322.9 1.6 copy-done.1
  324.6 3.9 fusion.12
  329.5 1.7 copy.23
  331.9 1.7 copy.22
  334.3 137.0 %all-reduce.9.cloned.1.call-done = f32[2,192,192]{2,1,0:T(8,128)} async-done(((f32[2,192,192]{2,1,0:T(8,128)}), f32[2,192,192]{2,1,0:T(8,128)}) %all-reduce.9.cloned.1.call-update) | async-done | bytes 294928 | tf_op jit(solution)/shard_map/psum | solution.py:48
  471.4 1.7 convolution_add_fusion.4
  473.1 1.6 convolution_add_fusion.3
  474.7 1.6 convolution_add_fusion.2
  477.7 4.1 convolution_bitcast_fusion
  481.9 64.5 %all-reduce.11.cloned.1.call-done = f32[2048,192]{0,1:T(8,128)} async-done(((f32[2048,192]{0,1:T(8,128)}), f32[2048,192]{0,1:T(8,128)}) %all-reduce.11.cloned.1.call-update) | async-done | bytes 1572880 | tf_op jit(solution)/shard_map/psum | solution.py:52
  546.3 1.6 constant_dynamic-slice_fusion
  (61 shorter events, 17.5 us)
Async XLA Ops:
  6.5 31.0 %copy-start = (f32[2,2048,192]{1,2,0:T(8,128)S(1)}, f32[2,2048,192]{1,2,0:T(8,128)}, u32[]{:S(2)}) copy-start(f32[2,2048,192]{1,2,0:T(8,128)} %param.4) | copy-start | bytes 9437188
  6.5 31.0 %all-gather.2.cloned.1.call-start = ((), (), s32[]{:S(2)}) async-start(), calls=%async_computation | async-start | bytes 1769472 | tf_op jit(solution)/shard_map/all_gather | solution.py:32
  7.3 182.5 %all-reduce.7.cloned.1.call-start = ((), (), s32[]{:S(2)}) async-start(), calls=%async_computation.1 | async-start | bytes 786432 | tf_op jit(solution)/shard_map/psum | solution.py:37
  42.6 428.8 %all-reduce.9.cloned.1.call-start = ((), (), s32[]{:S(2)}) async-start(), calls=%async_computation.2 | async-start | bytes 786432 | tf_op jit(solution)/shard_map/psum | solution.py:48
  192.6 117.7 %copy-start.4 = (f32[2,192,192]{2,1,0:T(8,128)S(1)}, f32[2,192,192]{2,1,0:T(8,128)}, u32[]{:S(2)}) copy-start(f32[2,192,192]{2,1,0:T(8,128)} %all-reduce.7.cloned.1.call-done) | copy-start | bytes 884740
  195.7 0.8 copy-start.6
  267.0 0.8 copy-start.5
  318.5 6.0 %copy-start.11 = (f32[2048]{0:T(1024)S(1)}, f32[2048]{0:T(1024)}, u32[]{:S(2)}) copy-start(f32[2048]{0:T(1024)} %param.6) | copy-start | bytes 24580
  322.9 1.6 copy-start.1
  324.6 146.8 %copy-start.7 = (f32[192,192]{1,0:T(8,128)S(1)}, f32[192,192]{1,0:T(8,128)}, u32[]{:S(2)}) copy-start(f32[192,192]{1,0:T(8,128)} %copy.25) | copy-start | bytes 442372
  324.6 146.8 %copy-start.8 = (f32[192,192]{1,0:T(8,128)S(1)}, f32[192,192]{1,0:T(8,128)}, u32[]{:S(2)}) copy-start(f32[192,192]{1,0:T(8,128)} %copy.26) | copy-start | bytes 442372
  328.5 217.9 %all-reduce.11.cloned.1.call-start = ((), (), s32[]{:S(2)}) async-start(), calls=%async_computation.3 | async-start | bytes 3145728 | tf_op jit(solution)/shard_map/psum | solution.py:52
  331.2 145.6 %copy-start.12 = (f32[2]{0:T(128)S(1)}, f32[2]{0:T(128)}, u32[]{:S(2)}) copy-start(f32[2]{0:T(128)} %param.7) | copy-start | bytes 28
  471.4 4.9 copy-start.3
  471.4 4.9 copy-start.10
  471.4 5.4 copy-start.9
  471.4 6.3 %copy-start.2 = (f32[2,2048,192]{1,2,0:T(8,128)S(1)}, f32[2,2048,192]{1,2,0:T(8,128)}, u32[]{:S(2)}) copy-start(f32[2,2048,192]{1,2,0:T(8,128)} %copy-done.1) | copy-start | bytes 9437188
Sparse Core Ops, SparseCore 0:
  9.2 28.2 all-gather.1
  42.7 146.9 all-reduce.6
  328.6 142.7 all-reduce.8
  482.0 64.2 all-reduce.10
where the time goes:
time: 558 us; the launch traced here: 554 us
  waiting for transfers between devices  374 us (67%)
  other arithmetic  112 us (20%)
  matrix products  37.4 us (7%)
  local copies, waits for them, and re-layouts  16.6 us (3%)
  between operations  13.4 us (2%)
    psum x1, waiting for transfers between devices, body(): cross_gram = lax.psum(cross_gram, 'cell')  146 us
    psum x1, waiting for transfers between devices, body(): curvature_gram = lax.psum(curvature_gram, 'cell')  137 us
    another operation x10, other arithmetic, invert(): factor = jnp.linalg.cholesky(normal_matrix)  64.8 us
    psum x1, waiting for transfers between devices, body(): summed = lax.psum(complete, 'samp')  64.5 us
    another operation x7, other arithmetic, invert(): return jax.scipy.linalg.cho_solve((factor, True), matrix.T)  44 us
    all_gather x1, waiting for transfers between devices, body(): panel_rows = lax.all_gather(reference_basis, 'samp', axis=0, tiled=True)  26.6 us
  transfers between devices with their start and end apart: 4, of which 4 were waited for; matrix products, arithmetic and copies ran while one was open for 2% of the time, Pallas kernels for 0%

commit v1 on v0

v1 whole, which is shorter than its diff:
```python
import functools

import jax
import jax.numpy as jnp
from jax import lax
from jax.experimental import pallas as pl
from jax.experimental.pallas import tpu as pltpu
from jax.sharding import PartitionSpec as P

NTERMS = 6
MESH = pl.DeviceIdType.MESH
F32, BF16 = jnp.float32, jnp.bfloat16
HIGHEST = lax.Precision.HIGHEST
NN = (((1,), (0,)), ((), ()))
NT = (((1,), (1,)), ((), ()))
LEAF = 64


def split(x):
    high = x.astype(BF16)
    return high, (x - high.astype(F32)).astype(BF16)


def dot(a, b, dims=NN):
    return lax.dot_general(a, b, dims, preferred_element_type=F32)


def dot3(a, b, dims=NN):
    (ah, al), (bh, bl) = a, b
    return dot(ah, bh, dims) + (dot(ah, bl, dims) + dot(al, bh, dims))


def matmul(a, b):
    return dot3(split(a), split(b))


def exact(a, b, dims=NN):
    return lax.dot_general(a, b, dims, precision=HIGHEST, preferred_element_type=F32)


def pack(first, second):
    middle = jnp.concatenate([first[:, 128:], second[:, 128:]], axis=1)
    return jnp.concatenate([first[:, :128], middle, second[:, :128]], axis=1)


def unpack(packed):
    middle = packed[:, 128:256]
    half = middle.shape[1] // 2
    first = jnp.concatenate([packed[:, :128], middle[:, :half]], axis=1)
    second = jnp.concatenate([packed[:, 256:384], middle[:, half:]], axis=1)
    return first, second


def sweep_leaf(leaf_ref):
    lane = lax.broadcasted_iota(jnp.int32, (8, 128), 1)
    row = lax.broadcasted_iota(jnp.int32, (8, 128), 0)
    within = lane & (LEAF - 1)
    start = lane - within

    def step(p, carry):
        first = 8 * p
        index = [start + first + c for c in range(8)]
        own = pl.ds(pl.multiple_of(first, 8), 8)
        pivot = leaf_ref[own, :]

        def column(x, c):
            return jnp.take_along_axis(x, index[c], axis=1, mode="promise_in_bounds")

        columns = [column(pivot, c) for c in range(8)]
        e = {
            (r, c): jnp.broadcast_to(columns[c][r : r + 1, :], (8, 128))
            for c in range(8)
            for r in range(c + 1)
        }

        def at(r, c):
            return (r, c) if r <= c else (c, r)

        for k in range(8):
            inverse = 1.0 / e[k, k]
            scaled = {j: e[at(k, j)] * inverse for j in range(8) if j != k}
            for j in range(8):
                for i in range(j + 1):
                    if i != k and j != k:
                        e[i, j] = e[i, j] - e[at(i, k)] * scaled[j]
            for j in scaled:
                e[at(k, j)] = scaled[j]
            e[k, k] = -inverse

        inside = (within >= first) & (within < first + 8)
        rows = [
            jnp.where(
                within == first + c,
                1.0,
                jnp.where(inside, 0.0, -jnp.broadcast_to(pivot[c : c + 1, :], (8, 128))),
            )
            for c in range(8)
        ]
        scaled_rows = []
        for r in range(8):
            total = e[at(r, 0)] * rows[0]
            for c in range(1, 8):
                total = total + e[at(r, c)] * rows[c]
            scaled_rows.append(total)
        for g in range(LEAF // 8):
            block = leaf_ref[8 * g : 8 * g + 8, :]
            total = jnp.where(inside, 0.0, block)
            for c in range(8):
                total = total - column(block, c) * scaled_rows[c]
            leaf_ref[8 * g : 8 * g + 8, :] = total
        joined = scaled_rows[0]
        for r in range(1, 8):
            joined = jnp.where(row == r, scaled_rows[r], joined)
        leaf_ref[own, :] = joined
        return carry

    lax.fori_loop(0, LEAF // 8, step, 0)


def invert(normal, leaf_ref, between):
    size = normal[0].shape[0]
    row = lax.broadcasted_iota(jnp.int32, (LEAF, size), 0)
    lane = lax.broadcasted_iota(jnp.int32, (LEAF, size), 1)
    every_lane = lax.broadcasted_iota(jnp.int32, (size, size), 1)
    for i in range(size // LEAF):
        own = slice(LEAF * i, LEAF * (i + 1))
        leaf_ref[...] = jnp.concatenate([n[own, own] for n in normal], axis=1)
        sweep_leaf(leaf_ref)
        if i == 0:
            between()
        minus_inverse = leaf_ref[...]
        updated = []
        for s, n in enumerate(normal):
            panel = jnp.where(
                lane == row + LEAF * i, 1.0, jnp.where((lane >= LEAF * i) & (lane < LEAF * (i + 1)), 0.0, -n[own, :])
            )
            scaled = exact(minus_inverse[:, LEAF * s : LEAF * (s + 1)], panel)
            kept = jnp.where((every_lane >= LEAF * i) & (every_lane < LEAF * (i + 1)), 0.0, n)
            new = kept - exact(n[:, own], scaled)
            parts = [new[: LEAF * i], scaled, new[LEAF * (i + 1) :]]
            updated.append(jnp.concatenate([part for part in parts if part.shape[0]], axis=0))
        normal = updated
    return normal


def series(curvature):
    size = curvature.shape[0]
    diagonal = lax.broadcasted_iota(jnp.int32, (size, size), 0) == lax.broadcasted_iota(jnp.int32, (size, size), 1)
    weight = [(-1.0) ** n / (2 * n + 1) for n in range(NTERMS)]

    def pair(n):
        return weight[n + 1] * curvature + jnp.where(diagonal, weight[n], 0.0)

    pieces = split(curvature)
    square = split(dot3(pieces, pieces))
    result = pair(NTERMS - 2)
    for n in range(NTERMS - 4, -1, -2):
        result = pair(n) + dot3(square, split(result))
    return result


def kernel(
    cells,
    depth,
    samps,
    bases_ref,
    own_ref,
    mass_ref,
    weight_ref,
    out_ref,
    gathered,
    zh,
    zl,
    gram,
    curv,
    c_own,
    c_in,
    c_all,
    g_own,
    g_in,
    g_all,
    leaf,
    lhs_h,
    lhs_l,
    pair_out,
    pair_in,
    sums,
    far_in,
    near_in,
    gather_send,
    gather_left,
    gather_right,
    gather_far,
    gather_pair,
    reduce_send,
    reduce_recv,
    final_send,
    final_pair,
    final_far,
    final_near,
):
    size, block = own_ref.shape
    half = size // 2
    groups = size // 8
    cell = lax.axis_index("cell")
    samp = lax.axis_index("samp")
    chips = samps // 2
    core = lax.rem(samp, 2)
    y = samp // 2

    def there(step):
        return lax.rem(y + step + chips, chips)

    def slot(step, other=False):
        return 2 * there(step) + (1 - core if other else core)

    partner, right, left = slot(0, True), slot(1), slot(-1)

    barrier = pltpu.get_barrier_semaphore()

    def greet(d, carry):
        pl.semaphore_signal(barrier, inc=1, device_id={"cell": lax.rem(cell + d, cells)}, device_id_type=MESH)
        return carry

    lax.fori_loop(1, cells, greet, 0)
    for friend in (partner, right, left):
        pl.semaphore_signal(barrier, inc=1, device_id={"samp": friend}, device_id_type=MESH)
    pl.semaphore_wait(barrier, cells + 2)

    def send(src, dst, send_sem, recv_sem, to):
        copy = pltpu.make_async_remote_copy(
            src_ref=src,
            dst_ref=dst,
            send_sem=send_sem,
            recv_sem=recv_sem,
            device_id={"samp": to},
            device_id_type=MESH,
        )
        copy.start()
        return copy

    def arrived(ref, sem):
        pltpu.make_async_copy(ref, ref, sem).wait()

    def rows(h):
        return pl.ds(half * h, half)

    sent = []
    mine = gathered.at[samp]
    for h in (0, 1):
        sent.append(send(own_ref.at[rows(h)], mine.at[rows(h)], gather_send.at[h], gather_left.at[h], right))
        sent.append(send(own_ref.at[rows(1 - h)], mine.at[rows(1 - h)], gather_send.at[3 - h], gather_right.at[1 - h], left))
    sent.append(send(own_ref, mine, gather_send.at[4], gather_pair.at[0], partner))

    def weights(j):
        return mass_ref[:, pl.ds(pl.multiple_of(j * block, block), block)] * (1.0 / depth)

    def own_gram(j, carry):
        columns = pl.ds(pl.multiple_of(j * block, block), block)
        mass = weights(j)
        for s in range(2):
            x = bases_ref[s, :, columns]
            xh, xl = split(x)
            at = pl.ds(size * (s + 1), size)
            zh[j, at, :] = xh
            zl[j, at, :] = xl
            term = dot3((xh, xl), split(x * mass), NT)
            curv[s] = jnp.where(j == 0, term, curv[s] + term)
        return carry

    curv[...] = jnp.zeros_like(curv)
    lax.fori_loop(0, samps, own_gram, 0)

    def cross(j, x, first=False):
        xh, xl = split(x)
        zh[j, pl.ds(0, size), :] = xh
        zl[j, pl.ds(0, size), :] = xl
        term = dot3((zh[j], zl[j]), split(x * weights(j)), NT)
        if first:
            gram[...] = term
        else:
            gram[...] += term

    cross(samp, own_ref[...], True)

    arrived(mine.at[rows(0)], gather_left.at[0])
    from_left, from_right, far = gathered.at[left], gathered.at[right], gathered.at[slot(2)]
    sent.append(send(from_left.at[rows(0)], from_left.at[rows(0)], gather_send.at[5], gather_far.at[0], right))
    arrived(mine.at[rows(1)], gather_right.at[1])
    sent.append(send(from_right.at[rows(1)], from_right.at[rows(1)], gather_send.at[6], gather_far.at[1], left))
    arrived(mine.at[rows(1)], gather_left.at[1])
    sent.append(send(from_left, from_left, gather_send.at[7], gather_pair.at[1], partner))
    arrived(mine.at[rows(0)], gather_right.at[0])
    sent.append(send(from_right, from_right, gather_send.at[8], gather_pair.at[2], partner))
    arrived(mine, gather_pair.at[0])
    cross(partner, gathered[partner])
    cross(left, gathered[left])
    cross(right, gathered[right])
    arrived(mine.at[rows(0)], gather_far.at[0])
    arrived(mine.at[rows(1)], gather_far.at[1])
    sent.append(send(far, far, gather_send.at[9], gather_pair.at[3], partner))
    cross(slot(2), gathered[slot(2)])
    for i, step in ((1, -1), (2, 1), (3, 2)):
        arrived(mine, gather_pair.at[i])
        cross(slot(step, True), gathered[slot(step, True)])

    line = 8
    per_line = groups * line // cells

    class Reduction:
        def __init__(self, own, incoming, whole, sem, shift):
            self.own, self.incoming, self.whole, self.shift = own, incoming, whole, shift
            self.scatter_send, self.scatter_recv = reduce_send.at[sem], reduce_recv.at[sem]
            self.share_send, self.share_recv = reduce_send.at[sem + 1], reduce_recv.at[sem + 1]
            self.owns = self.is_owner(cell)

        def is_owner(self, c):
            z = lax.rem(c, line) - self.shift
            return (z >= 0) & (z < per_line)

        def group(self, c):
            return pl.ds(pl.multiple_of(8 * ((c // line) * per_line + lax.rem(c, line) - self.shift), 8), 8)

        def scatter(self):
            def one(d, carry):
                to = lax.rem(cell + d, cells)

                @pl.when(self.is_owner(to))
                def _():
                    pltpu.make_async_remote_copy(
                        src_ref=self.own.at[self.group(to)],
                        dst_ref=self.incoming.at[cell],
                        send_sem=self.scatter_send,
                        recv_sem=self.scatter_recv,
                        device_id={"cell": to},
                        device_id_type=MESH,
                    ).start()

                return carry

            lax.fori_loop(1, cells, one, 0)

        def share(self):
            @pl.when(self.owns)
            def _():
                self.incoming[cell] = self.own[self.group(cell), :]
                others = self.incoming.at[pl.ds(0, cells - 1)]
                arrived(others, self.scatter_recv)
                self.whole[self.group(cell), :] = jnp.sum(self.incoming[...], axis=0)

                def one(d, carry):
                    pltpu.make_async_remote_copy(
                        src_ref=self.whole.at[self.group(cell)],
                        dst_ref=self.whole.at[self.group(cell)],
                        send_sem=self.share_send,
                        recv_sem=self.share_recv,
                        device_id={"cell": lax.rem(cell + d, cells)},
                        device_id_type=MESH,
                    ).start()
                    return carry

                lax.fori_loop(1, cells, one, 0)

        def either(self, sem):
            @pl.when(self.owns)
            def _():
                arrived(self.own.at[pl.ds(0, size - 8)], sem)

            @pl.when(jnp.logical_not(self.owns))
            def _():
                arrived(self.own, sem)

        def finish(self):
            self.either(self.share_recv)

        def drain(self):
            self.either(self.scatter_send)

            @pl.when(self.owns)
            def _():
                arrived(self.incoming.at[pl.ds(0, cells - 1)], self.share_send)

    reduce_c = Reduction(c_own, c_in, c_all, 0, 0)
    reduce_g = Reduction(g_own, g_in, g_all, 2, line - per_line)

    c_own[...] = pack(gram[size : 2 * size], gram[2 * size :])
    reduce_c.scatter()
    g_own[:, :384] = pack(curv[0], curv[1])
    g_own[:, 384:] = gram[:size]
    reduce_g.scatter()
    reduce_c.share()
    reduce_c.finish()

    cross_t = unpack(c_all[...])
    normal = [exact(c, c, NT) for c in cross_t]
    minus_inverse = invert(normal, leaf, reduce_g.share)
    inverses = [-exact(m, c) for m, c in zip(minus_inverse, cross_t)]

    reduce_g.finish()
    of_bases = unpack(g_all[:, :384])
    of_reference = g_all[:, 384:]
    plain = jnp.zeros((size, size), F32)
    for s in range(2):
        x = split(inverses[s])
        turned = inverses[s].T
        middle = dot3(split(of_bases[s]), x) - 2.0 * cross_t[s]
        curvature = matmul(turned, middle) + of_reference
        factors = series(curvature) * weight_ref[s]
        plain = plain - factors
        lhs_h[s + 1], lhs_l[s + 1] = split(matmul(factors, turned))
    lhs_h[0], lhs_l[0] = split(plain)

    def term(j):
        total = None
        for k in range(3):
            at = pl.ds(size * k, size)
            part = dot3((lhs_h[k], lhs_l[k]), (zh[j, at, :], zl[j, at, :]))
            total = part if total is None else total + part
        return total

    steps = (2, 1, -1, 0)
    for i, step in enumerate(steps):
        pair_out[i] = term(slot(step, True))
        sent.append(send(pair_out.at[i], pair_in.at[i], final_send.at[i], final_pair.at[i], partner))

    def own_term(i):
        value = term(slot(steps[i]))
        arrived(pair_in.at[i], final_pair.at[i])
        return value + pair_in[i]

    def forward(i, h, to, sem, recv, dst):
        sent.append(send(sums.at[i, rows(h)], dst, final_send.at[sem], recv, to))

    sums[0] = own_term(0)
    forward(0, 0, right, 4, final_far.at[0], far_in.at[0])
    forward(0, 1, left, 5, final_far.at[1], far_in.at[1])
    sums[1] = own_term(1)
    forward(1, 1, right, 6, final_near.at[1], near_in.at[0, rows(1)])
    sums[2] = own_term(2)
    forward(2, 0, left, 7, final_near.at[2], near_in.at[1, rows(0)])
    arrived(far_in.at[0], final_far.at[0])
    sums[1, rows(0), :] += far_in[0]
    forward(1, 0, right, 8, final_near.at[0], near_in.at[0, rows(0)])
    arrived(far_in.at[1], final_far.at[1])
    sums[2, rows(1), :] += far_in[1]
    forward(2, 1, left, 9, final_near.at[3], near_in.at[1, rows(1)])
    out_ref[...] = own_term(3)
    for i in range(4):
        arrived(far_in.at[0], final_near.at[i])
    out_ref[...] += near_in[0] + near_in[1]

    for copy in sent:
        copy.wait_send()
    reduce_c.drain()
    reduce_g.drain()


def body(bases, reference_basis, mass, interp_weights):
    cells, samps = lax.axis_size("cell"), lax.axis_size("samp")
    count, depth, size = bases.shape
    block = reference_basis.shape[0]
    packed, wide = 2 * size, 3 * size
    half = size // 2
    vmem = pl.BlockSpec(memory_space=pltpu.VMEM)
    result = pl.pallas_call(
        functools.partial(kernel, cells, depth * cells, samps),
        out_shape=jax.ShapeDtypeStruct((size, block), F32),
        in_specs=[vmem, vmem, vmem, pl.BlockSpec(memory_space=pltpu.SMEM)],
        out_specs=vmem,
        scratch_shapes=[
            pltpu.VMEM((samps, size, block), F32),
            pltpu.VMEM((samps, 3 * size, block), BF16),
            pltpu.VMEM((samps, 3 * size, block), BF16),
            pltpu.VMEM((3 * size, size), F32),
            pltpu.VMEM((2, size, size), F32),
            pltpu.VMEM((size, packed), F32),
            pltpu.VMEM((cells, 8, packed), F32),
            pltpu.VMEM((size, packed), F32),
            pltpu.VMEM((size, wide), F32),
            pltpu.VMEM((cells, 8, wide), F32),
            pltpu.VMEM((size, wide), F32),
            pltpu.VMEM((LEAF, 2 * LEAF), F32),
            pltpu.VMEM((3, size, size), BF16),
            pltpu.VMEM((3, size, size), BF16),
            pltpu.VMEM((4, size, block), F32),
            pltpu.VMEM((4, size, block), F32),
            pltpu.VMEM((3, size, block), F32),
            pltpu.VMEM((2, half, block), F32),
            pltpu.VMEM((2, size, block), F32),
            pltpu.SemaphoreType.DMA((10,)),
            pltpu.SemaphoreType.DMA((2,)),
            pltpu.SemaphoreType.DMA((2,)),
            pltpu.SemaphoreType.DMA((2,)),
            pltpu.SemaphoreType.DMA((4,)),
            pltpu.SemaphoreType.DMA((4,)),
            pltpu.SemaphoreType.DMA((4,)),
            pltpu.SemaphoreType.DMA((10,)),
            pltpu.SemaphoreType.DMA((4,)),
            pltpu.SemaphoreType.DMA((2,)),
            pltpu.SemaphoreType.DMA((4,)),
        ],
        compiler_params=pltpu.CompilerParams(
            collective_id=0, has_side_effects=True, vmem_limit_bytes=48 * 1024 * 1024
        ),
    )(jnp.swapaxes(bases, 1, 2), reference_basis.T, mass[None, :], interp_weights)
    return result.T


def solution(mesh):
    placed = (P("samp", "cell", None), P(("cell", "samp"), None), P("cell"), P("samp"))
    return jax.shard_map(
        body, mesh=mesh, in_specs=placed, out_specs=P(("cell", "samp"), None), check_vma=False
    )
```

time: 558 us -> 94.9 us (0.17)
  waiting for transfers between devices: 374 us -> 0 us
  other arithmetic: 112 us -> 0 us
  Pallas kernels: 0 us -> 89.9 us
  matrix products: 37.4 us -> 0 us
  between operations: 13.4 us -> 0.01 us
  local copies, waits for them, and re-layouts: 16.6 us -> 4.85 us
    psum x3 -> x0, waiting for transfers between devices: 347 us -> none  [the longest x1 146 us: body(): cross_gram = lax.psum(cross_gram, 'cell')]
    another operation x17 -> x0, other arithmetic: 109 us -> none  [the longest x10 64.8 us: invert(): factor = jnp.linalg.cholesky(normal_matrix)]
    pallas_call x0 -> x1, Pallas kernels: none -> 89.9 us  [body(): pl.pallas_call(functools.partial(kernel, cells, depth * cells, samps), ou...]
    all_gather x1 -> x0, waiting for transfers between devices: 26.6 us -> none  [body(): panel_rows = lax.all_gather(reference_basis, 'samp', axis=0, tiled=True)]
    dot_general x10 -> x0, matrix products: 26.4 us -> none  [the longest x5 6.24 us: series(): jnp.matmul(curvature_gram, result, precision=HIGHEST_PRECISION)]
    another operation x8 -> x0, matrix products: 11 us -> none  [the longest x6 7.47 us: invert(): return jax.scipy.linalg.cho_solve((factor, True), matrix.T)]
    mul x5 -> x0, local copies, waits for them, and re-layouts: 5.87 us -> none  [the longest x4 5.08 us: series(): identity * ((-1.0) ** degree / (2 * degree + 1))]
  transfers between devices with their start and end apart: 4 -> 0, of which waited for: 4 -> 0; matrix products, arithmetic and copies ran while one was open for 2% -> 0% of each run, Pallas kernels for 0% -> 0%
where the time goes in v1:
time: 94.9 us; the launch traced here: 94.7 us
  Pallas kernels  89.9 us (95%)
  local copies, waits for them, and re-layouts  4.85 us (5%)
    pallas_call x1, Pallas kernels, body(): pl.pallas_call(functools.partial(kernel, cells, depth * cells, samps), ou...  89.9 us
    unnamed x9, local copies, waits for them, and re-layouts  4.85 us

profile of v1, /device:TPU:8, one launch (start us, length us, event | category | flops | bytes accessed | tf_op | source)
XLA Modules:
  0.0 94.7 jit_solution(8431967752739665124)
XLA Ops:
  0.0 0.0 copy-start
  0.0 1.9 %copy-done = f32[2,2048,192]{1,2,0:T(8,128)S(1)} copy-done((f32[2,2048,192]{1,2,0:T(8,128)S(1)}, f32[2,2048,192]{1,2,0:T(8,128)}, u32[]{:S(2)}) %copy-start) | copy-done | bytes 3145752
  1.9 0.0 copy-start.1
  1.9 0.9 copy-done.1
  2.8 0.0 copy-start.2
  2.8 0.7 copy-done.2
  3.5 0.0 copy-start.3
  3.5 0.7 copy-done.3
  4.2 89.9 %shard_map.46 = f32[192,256]{1,0:T(8,128)S(1)} custom-call(f32[2,192,2048]{2,1,0:T(8,128)S(1)} %bitcast.4, f32[192,256]{1,0:T(8,128)S(1)} %bitcast.6, f32[1,2048]{1,0:T(1,128)S(1)} %bitcast.7, f32[2]{0:T(128)S(1)} %copy-done.3), custom_call_target="tpu_custom_call" | custom-call | tf_op jit(solution)/shard_map/pallas_call | solution.py:465
  94.0 0.7 copy.6
Async XLA Ops:
  0.0 1.9 %copy-start = (f32[2,2048,192]{1,2,0:T(8,128)S(1)}, f32[2,2048,192]{1,2,0:T(8,128)}, u32[]{:S(2)}) copy-start(f32[2,2048,192]{1,2,0:T(8,128)} %param.4) | copy-start | bytes 9437188
  1.9 0.9 copy-start.1
  2.8 0.7 copy-start.2
  3.5 0.7 copy-start.3

commit v2 on v1

--- a/solution.py
+++ b/solution.py
@@ -163,11 +163,14 @@
     cells,
     depth,
     samps,
-    bases_ref,
-    own_ref,
-    mass_ref,
+    bases_hbm,
+    own_hbm,
+    mass_hbm,
+    weight_hbm,
+    out_ref,
+    bases,
+    mass_row,
     weight_ref,
-    out_ref,
     gathered,
     zh,
     zl,
@@ -177,7 +180,10 @@
     c_in,
     c_all,
     g_own,
-    g_in,
+    g_x,
+    g_part,
+    g_z,
+    h_in,
     g_all,
     leaf,
     lhs_h,
@@ -187,6 +193,7 @@
     sums,
     far_in,
     near_in,
+    load_sem,
     gather_send,
     gather_left,
     gather_right,
@@ -199,14 +206,16 @@
     final_far,
     final_near,
 ):
-    size, block = own_ref.shape
+    size, block = own_hbm.shape
     half = size // 2
-    groups = size // 8
     cell = lax.axis_index("cell")
     samp = lax.axis_index("samp")
     chips = samps // 2
     core = lax.rem(samp, 2)
     y = samp // 2
+    line = 8
+    lines = cells // line
+    x, z = cell // line, lax.rem(cell, line)
 
     def there(step):
         return lax.rem(y + step + chips, chips)
@@ -216,73 +225,230 @@
 
     partner, right, left = slot(0, True), slot(1), slot(-1)
 
+    def other_cell(d):
+        return lax.rem(cell + d, cells)
+
+    def other_samp(d):
+        return lax.rem(samp + d, samps)
+
     barrier = pltpu.get_barrier_semaphore()
-
-    def greet(d, carry):
-        pl.semaphore_signal(barrier, inc=1, device_id={"cell": lax.rem(cell + d, cells)}, device_id_type=MESH)
-        return carry
-
-    lax.fori_loop(1, cells, greet, 0)
-    for friend in (partner, right, left):
-        pl.semaphore_signal(barrier, inc=1, device_id={"samp": friend}, device_id_type=MESH)
-    pl.semaphore_wait(barrier, cells + 2)
-
-    def send(src, dst, send_sem, recv_sem, to):
-        copy = pltpu.make_async_remote_copy(
-            src_ref=src,
-            dst_ref=dst,
-            send_sem=send_sem,
-            recv_sem=recv_sem,
-            device_id={"samp": to},
-            device_id_type=MESH,
-        )
-        copy.start()
-        return copy
-
-    def arrived(ref, sem):
-        pltpu.make_async_copy(ref, ref, sem).wait()
-
-    def rows(h):
-        return pl.ds(half * h, half)
-
-    sent = []
+    for d in range(1, samps):
+        pl.semaphore_signal(barrier, inc=1, device_id={"samp": other_samp(d)}, device_id_type=MESH)
+    for d in range(1, cells):
+        pl.semaphore_signal(barrier, inc=1, device_id={"cell": other_cell(d)}, device_id_type=MESH)
+
+    def columns(j):
+        return pl.ds(pl.multiple_of(j * block, block), block)
+
+    def load_bases(j):
+        at = bases.at[:, :, columns(j)]
+        return pltpu.make_async_copy(bases_hbm.at[:, :, columns(j)], at, load_sem.at[j])
+
+    loads = [
+        pltpu.make_async_copy(mass_hbm, mass_row, load_sem.at[samps]),
+        pltpu.make_async_copy(own_hbm, gathered.at[samp], load_sem.at[samps + 1]),
+        pltpu.make_async_copy(weight_hbm, weight_ref, load_sem.at[samps + 2]),
+    ]
+    for load in loads:
+        load.start()
+    for j in range(samps):
+        load_bases(j).start()
+
+    def weights(j):
+        return mass_row[:, columns(j)] * (1.0 / depth)
+
+    for load in loads:
+        load.wait()
     mine = gathered.at[samp]
-    for h in (0, 1):
-        sent.append(send(own_ref.at[rows(h)], mine.at[rows(h)], gather_send.at[h], gather_left.at[h], right))
-        sent.append(send(own_ref.at[rows(1 - h)], mine.at[rows(1 - h)], gather_send.at[3 - h], gather_right.at[1 - h], left))
-    sent.append(send(own_ref, mine, gather_send.at[4], gather_pair.at[0], partner))
-
-    def weights(j):
-        return mass_ref[:, pl.ds(pl.multiple_of(j * block, block), block)] * (1.0 / depth)
+    reference = mine[...]
+    g_own[:, 2 * size :] = dot3(split(reference), split(reference * weights(samp)), NT)
 
     def own_gram(j, carry):
-        columns = pl.ds(pl.multiple_of(j * block, block), block)
+        load_bases(j).wait()
         mass = weights(j)
         for s in range(2):
-            x = bases_ref[s, :, columns]
-            xh, xl = split(x)
+            value = bases[s, :, columns(j)]
+            high, low = split(value)
             at = pl.ds(size * (s + 1), size)
-            zh[j, at, :] = xh
-            zl[j, at, :] = xl
-            term = dot3((xh, xl), split(x * mass), NT)
-            curv[s] = jnp.where(j == 0, term, curv[s] + term)
+            zh[j, at, :] = high
+            zl[j, at, :] = low
+            curv[s] += dot3((high, low), split(value * mass), NT)
         return carry
 
     curv[...] = jnp.zeros_like(curv)
     lax.fori_loop(0, samps, own_gram, 0)
-
-    def cross(j, x, first=False):
-        xh, xl = split(x)
-        zh[j, pl.ds(0, size), :] = xh
-        zl[j, pl.ds(0, size), :] = xl
-        term = dot3((zh[j], zl[j]), split(x * weights(j)), NT)
+    g_own[:, : 2 * size] = pack(curv[0], curv[1])
+
+    def cross(j, first=False):
+        value = gathered[j]
+        high, low = split(value)
+        zh[j, pl.ds(0, size), :] = high
+        zl[j, pl.ds(0, size), :] = low
+        at = pl.ds(size, 2 * size)
+        term = dot3((zh[j, at, :], zl[j, at, :]), split(value * weights(j)), NT)
         if first:
             gram[...] = term
         else:
             gram[...] += term
 
-    cross(samp, own_ref[...], True)
-
+    cross(samp, True)
+
+    pl.semaphore_wait(barrier, cells + samps - 2)
+
+    def remote(src, dst, send_sem, recv_sem, **to):
+        copy = pltpu.make_async_remote_copy(
+            src_ref=src, dst_ref=dst, send_sem=send_sem, recv_sem=recv_sem, device_id=to, device_id_type=MESH
+        )
+        copy.start()
+        return copy
+
+    def send(src, dst, send_sem, recv_sem, to):
+        return remote(src, dst, send_sem, recv_sem, samp=to)
+
+    def arrived(ref, sem):
+        pltpu.make_async_copy(ref, ref, sem).wait()
+
+    def rows(h):
+        return pl.ds(half * h, half)
+
+    sent = []
+    for h in (0, 1):
+        sent.append(send(mine.at[rows(h)], mine.at[rows(h)], gather_send.at[h], gather_left.at[h], right))
+        sent.append(send(mine.at[rows(1 - h)], mine.at[rows(1 - h)], gather_send.at[3 - h], gather_right.at[1 - h], left))
+    sent.append(send(mine, mine, gather_send.at[4], gather_pair.at[0], partner))
+
+    quarter = size // lines
+    owns_g = z < quarter // 8
+
+    def g_rows(x_of, z_of=None):
+        if z_of is None:
+            return pl.ds(pl.multiple_of(quarter * x_of, 8), quarter)
+        return pl.ds(pl.multiple_of(quarter * x_of + 8 * z_of, 8), 8)
+
+    def count_rows(n):
+        return g_own.at[pl.ds(0, n)]
+
+    def g_scatter_x():
+        for d in range(1, lines):
+            to = lax.rem(x + d, lines)
+            remote(g_own.at[g_rows(to)], g_x.at[x], reduce_send.at[0], reduce_recv.at[0], cell=to * line + z)
+
+    def g_scatter_z():
+        g_x[x] = g_own[g_rows(x), :]
+        arrived(count_rows(quarter * (lines - 1)), reduce_recv.at[0])
+        g_part[...] = jnp.sum(g_x[...], axis=0)
+        for d in range(1, line):
+            to = lax.rem(z + d, line)
+
+            @pl.when(to < quarter // 8)
+            def _(to=to):
+                src = g_part.at[pl.ds(pl.multiple_of(8 * to, 8), 8)]
+                remote(src, g_z.at[z], reduce_send.at[1], reduce_recv.at[1], cell=x * line + to)
+
+    def g_scatter_samp():
+        @pl.when(owns_g)
+        def _():
+            g_z[z] = g_part[pl.ds(pl.multiple_of(8 * z, 8), 8), :]
+            arrived(count_rows(8 * (line - 1)), reduce_recv.at[1])
+            total = jnp.sum(g_z[...], axis=0)
+            g_all[g_rows(x, z), : 2 * size] = total[:, : 2 * size]
+            h_in[samp] = total[:, 2 * size :]
+            for d in range(1, samps):
+                remote(h_in.at[samp], h_in.at[samp], reduce_send.at[2], reduce_recv.at[2], samp=other_samp(d))
+
+    def g_share_z():
+        @pl.when(owns_g)
+        def _():
+            arrived(h_in.at[pl.ds(0, samps - 1)], reduce_recv.at[2])
+            g_all[g_rows(x, z), 2 * size :] = jnp.sum(h_in[...], axis=0)
+            piece = g_all.at[g_rows(x, z)]
+            for d in range(1, line):
+                to = lax.rem(z + d, line)
+                remote(piece, piece, reduce_send.at[3], reduce_recv.at[3], cell=x * line + to)
+
+    def g_counted(owner, rest, sem):
+        @pl.when(owns_g)
+        def _():
+            arrived(count_rows(owner), sem)
+
+        if rest:
+
+            @pl.when(jnp.logical_not(owns_g))
+            def _():
+                arrived(count_rows(rest), sem)
+
+    def g_share_x():
+        g_counted(quarter - 8, quarter, reduce_recv.at[3])
+        piece = g_all.at[g_rows(x)]
+        for d in range(1, lines):
+            to = lax.rem(x + d, lines)
+            remote(piece, piece, reduce_send.at[4], reduce_recv.at[4], cell=to * line + z)
+
+    def g_finish():
+        arrived(count_rows(quarter * (lines - 1)), reduce_recv.at[4])
+
+    def g_drain():
+        arrived(count_rows(quarter * (lines - 1)), reduce_send.at[0])
+        g_counted(quarter - 8, quarter, reduce_send.at[1])
+
+        @pl.when(owns_g)
+        def _():
+            arrived(h_in.at[pl.ds(0, samps - 1)], reduce_send.at[2])
+
+        g_counted(8 * (line - 1), 0, reduce_send.at[3])
+        arrived(count_rows(quarter * (lines - 1)), reduce_send.at[4])
+
+    group = 16
+    per_line = size // group // lines
+    z_pair = z // 2
+    owns_c = (lax.rem(z, 2) == lax.rem(x + core, 2)) & (z_pair < per_line)
+
+    def c_rows(x_of, pair_of):
+        return pl.ds(pl.multiple_of(group * (per_line * x_of + pair_of), group), group)
+
+    def c_scatter():
+        for dx in range(lines):
+            to_x = lax.rem(x + dx, lines)
+            for dq in range(per_line):
+                to_pair = lax.rem(z_pair + dq, per_line)
+                to = to_x * line + 2 * to_pair + lax.rem(to_x + core, 2)
+
+                def one(to=to, to_x=to_x, to_pair=to_pair):
+                    src = c_own.at[c_rows(to_x, to_pair)]
+                    remote(src, c_in.at[cell], reduce_send.at[5], reduce_recv.at[5], cell=to)
+
+                if dx:
+                    one()
+                else:
+                    pl.when(to != cell)(one)
+
+    def c_share():
+        @pl.when(owns_c)
+        def _():
+            here = c_rows(x, z_pair)
+            c_in[cell] = c_own[here, :]
+            arrived(c_in.at[pl.ds(0, cells - 1)], reduce_recv.at[5])
+            c_all[here, :] = jnp.sum(c_in[...], axis=0)
+            for d in range(1, cells):
+                remote(c_all.at[here], c_all.at[here], reduce_send.at[6], reduce_recv.at[6], cell=other_cell(d))
+
+    def c_counted(sem):
+        @pl.when(owns_c)
+        def _():
+            arrived(c_own.at[pl.ds(0, size - group)], sem)
+
+        @pl.when(jnp.logical_not(owns_c))
+        def _():
+            arrived(c_own, sem)
+
+    def c_drain():
+        c_counted(reduce_send.at[5])
+
+        @pl.when(owns_c)
+        def _():
+            arrived(c_in.at[pl.ds(0, cells - 1)], reduce_send.at[6])
+
+    g_scatter_x()
     arrived(mine.at[rows(0)], gather_left.at[0])
     from_left, from_right, far = gathered.at[left], gathered.at[right], gathered.at[slot(2)]
     sent.append(send(from_left.at[rows(0)], from_left.at[rows(0)], gather_send.at[5], gather_far.at[0], right))
@@ -293,117 +459,38 @@
     arrived(mine.at[rows(0)], gather_right.at[0])
     sent.append(send(from_right, from_right, gather_send.at[8], gather_pair.at[2], partner))
     arrived(mine, gather_pair.at[0])
-    cross(partner, gathered[partner])
-    cross(left, gathered[left])
-    cross(right, gathered[right])
+    cross(partner)
+    cross(left)
+    cross(right)
+    g_scatter_z()
     arrived(mine.at[rows(0)], gather_far.at[0])
     arrived(mine.at[rows(1)], gather_far.at[1])
     sent.append(send(far, far, gather_send.at[9], gather_pair.at[3], partner))
-    cross(slot(2), gathered[slot(2)])
+    cross(slot(2))
     for i, step in ((1, -1), (2, 1), (3, 2)):
         arrived(mine, gather_pair.at[i])
-        cross(slot(step, True), gathered[slot(step, True)])
-
-    line = 8
-    per_line = groups * line // cells
-
-    class Reduction:
-        def __init__(self, own, incoming, whole, sem, shift):
-            self.own, self.incoming, self.whole, self.shift = own, incoming, whole, shift
-            self.scatter_send, self.scatter_recv = reduce_send.at[sem], reduce_recv.at[sem]
-            self.share_send, self.share_recv = reduce_send.at[sem + 1], reduce_recv.at[sem + 1]
-            self.owns = self.is_owner(cell)
-
-        def is_owner(self, c):
-            z = lax.rem(c, line) - self.shift
-            return (z >= 0) & (z < per_line)
-
-        def group(self, c):
-            return pl.ds(pl.multiple_of(8 * ((c // line) * per_line + lax.rem(c, line) - self.shift), 8), 8)
-
-        def scatter(self):
-            def one(d, carry):
-                to = lax.rem(cell + d, cells)
-
-                @pl.when(self.is_owner(to))
-                def _():
-                    pltpu.make_async_remote_copy(
-                        src_ref=self.own.at[self.group(to)],
-                        dst_ref=self.incoming.at[cell],
-                        send_sem=self.scatter_send,
-                        recv_sem=self.scatter_recv,
-                        device_id={"cell": to},
-                        device_id_type=MESH,
-                    ).start()
-
-                return carry
-
-            lax.fori_loop(1, cells, one, 0)
-
-        def share(self):
-            @pl.when(self.owns)
-            def _():
-                self.incoming[cell] = self.own[self.group(cell), :]
-                others = self.incoming.at[pl.ds(0, cells - 1)]
-                arrived(others, self.scatter_recv)
-                self.whole[self.group(cell), :] = jnp.sum(self.incoming[...], axis=0)
-
-                def one(d, carry):
-                    pltpu.make_async_remote_copy(
-                        src_ref=self.whole.at[self.group(cell)],
-                        dst_ref=self.whole.at[self.group(cell)],
-                        send_sem=self.share_send,
-                        recv_sem=self.share_recv,
-                        device_id={"cell": lax.rem(cell + d, cells)},
-                        device_id_type=MESH,
-                    ).start()
-                    return carry
-
-                lax.fori_loop(1, cells, one, 0)
-
-        def either(self, sem):
-            @pl.when(self.owns)
-            def _():
-                arrived(self.own.at[pl.ds(0, size - 8)], sem)
-
-            @pl.when(jnp.logical_not(self.owns))
-            def _():
-                arrived(self.own, sem)
-
-        def finish(self):
-            self.either(self.share_recv)
-
-        def drain(self):
-            self.either(self.scatter_send)
-
-            @pl.when(self.owns)
-            def _():
-                arrived(self.incoming.at[pl.ds(0, cells - 1)], self.share_send)
-
-    reduce_c = Reduction(c_own, c_in, c_all, 0, 0)
-    reduce_g = Reduction(g_own, g_in, g_all, 2, line - per_line)
-
-    c_own[...] = pack(gram[size : 2 * size], gram[2 * size :])
-    reduce_c.scatter()
-    g_own[:, :384] = pack(curv[0], curv[1])
-    g_own[:, 384:] = gram[:size]
-    reduce_g.scatter()
-    reduce_c.share()
-    reduce_c.finish()
+        cross(slot(step, True))
+
+    c_own[...] = pack(gram[:size], gram[size:])
+    c_scatter()
+    g_scatter_samp()
+    c_share()
+    g_share_z()
+    c_counted(reduce_recv.at[6])
 
     cross_t = unpack(c_all[...])
     normal = [exact(c, c, NT) for c in cross_t]
-    minus_inverse = invert(normal, leaf, reduce_g.share)
+    minus_inverse = invert(normal, leaf, g_share_x)
     inverses = [-exact(m, c) for m, c in zip(minus_inverse, cross_t)]
 
-    reduce_g.finish()
-    of_bases = unpack(g_all[:, :384])
-    of_reference = g_all[:, 384:]
+    g_finish()
+    of_bases = unpack(g_all[:, : 2 * size])
+    of_reference = g_all[:, 2 * size :]
     plain = jnp.zeros((size, size), F32)
     for s in range(2):
-        x = split(inverses[s])
+        inverse = split(inverses[s])
         turned = inverses[s].T
-        middle = dot3(split(of_bases[s]), x) - 2.0 * cross_t[s]
+        middle = dot3(split(of_bases[s]), inverse) - 2.0 * cross_t[s]
         curvature = matmul(turned, middle) + of_reference
         factors = series(curvature) * weight_ref[s]
         plain = plain - factors
@@ -451,8 +538,8 @@
 
     for copy in sent:
         copy.wait_send()
-    reduce_c.drain()
-    reduce_g.drain()
+    c_drain()
+    g_drain()
 
 
 def body(bases, reference_basis, mass, interp_weights):
@@ -461,23 +548,31 @@
     block = reference_basis.shape[0]
     packed, wide = 2 * size, 3 * size
     half = size // 2
-    vmem = pl.BlockSpec(memory_space=pltpu.VMEM)
+    hbm, vmem = pl.BlockSpec(memory_space=pltpu.HBM), pl.BlockSpec(memory_space=pltpu.VMEM)
+    line, group = 8, 16
+    lines = cells // line
     result = pl.pallas_call(
         functools.partial(kernel, cells, depth * cells, samps),
         out_shape=jax.ShapeDtypeStruct((size, block), F32),
-        in_specs=[vmem, vmem, vmem, pl.BlockSpec(memory_space=pltpu.SMEM)],
+        in_specs=[hbm] * 4,
         out_specs=vmem,
         scratch_shapes=[
+            pltpu.VMEM((count, size, depth), F32),
+            pltpu.VMEM((1, depth), F32),
+            pltpu.SMEM((count,), F32),
             pltpu.VMEM((samps, size, block), F32),
             pltpu.VMEM((samps, 3 * size, block), BF16),
             pltpu.VMEM((samps, 3 * size, block), BF16),
-            pltpu.VMEM((3 * size, size), F32),
+            pltpu.VMEM((packed, size), F32),
             pltpu.VMEM((2, size, size), F32),
             pltpu.VMEM((size, packed), F32),
-            pltpu.VMEM((cells, 8, packed), F32),
+            pltpu.VMEM((cells, group, packed), F32),
             pltpu.VMEM((size, packed), F32),
             pltpu.VMEM((size, wide), F32),
-            pltpu.VMEM((cells, 8, wide), F32),
+            pltpu.VMEM((lines, size // lines, wide), F32),
+            pltpu.VMEM((size // lines, wide), F32),
+            pltpu.VMEM((line, 8, wide), F32),
+            pltpu.VMEM((samps, 8, size), F32),
             pltpu.VMEM((size, wide), F32),
             pltpu.VMEM((LEAF, 2 * LEAF), F32),
             pltpu.VMEM((3, size, size), BF16),
@@ -487,13 +582,14 @@
             pltpu.VMEM((3, size, block), F32),
             pltpu.VMEM((2, half, block), F32),
             pltpu.VMEM((2, size, block), F32),
+            pltpu.SemaphoreType.DMA((samps + 3,)),
             pltpu.SemaphoreType.DMA((10,)),
             pltpu.SemaphoreType.DMA((2,)),
             pltpu.SemaphoreType.DMA((2,)),
             pltpu.SemaphoreType.DMA((2,)),
             pltpu.SemaphoreType.DMA((4,)),
-            pltpu.SemaphoreType.DMA((4,)),
-            pltpu.SemaphoreType.DMA((4,)),
+            pltpu.SemaphoreType.DMA((7,)),
+            pltpu.SemaphoreType.DMA((7,)),
             pltpu.SemaphoreType.DMA((10,)),
             pltpu.SemaphoreType.DMA((4,)),
             pltpu.SemaphoreType.DMA((2,)),

time: 94.9 us -> 77.5 us (0.82)
  Pallas kernels: 89.9 us -> 72.5 us
    pallas_call x1, Pallas kernels: 89.9 us -> 72.5 us  [body(): pl.pallas_call(functools.partial(kernel, cells, depth * cells, samps), ou...]
where the time goes in v2:
time: 77.5 us; the launch traced here: 77.3 us
  Pallas kernels  72.5 us (94%)
  local copies, waits for them, and re-layouts  4.85 us (6%)
    pallas_call x1, Pallas kernels, body(): pl.pallas_call(functools.partial(kernel, cells, depth * cells, samps), ou...  72.5 us
    unnamed x9, local copies, waits for them, and re-layouts  4.85 us

profile of v2, /device:TPU:8, one launch (start us, length us, event | category | flops | bytes accessed | tf_op | source)
XLA Modules:
  0.0 77.3 jit_solution(14763885100484215466)
XLA Ops:
  0.0 0.0 copy-start
  0.0 1.9 %copy-done = f32[2,2048,192]{1,2,0:T(8,128)S(1)} copy-done((f32[2,2048,192]{1,2,0:T(8,128)S(1)}, f32[2,2048,192]{1,2,0:T(8,128)}, u32[]{:S(2)}) %copy-start) | copy-done | bytes 3145752
  1.9 0.0 copy-start.1
  1.9 0.9 %copy-done.1 = f32[256,192]{0,1:T(8,128)S(1)} copy-done((f32[256,192]{0,1:T(8,128)S(1)}, f32[256,192]{0,1:T(8,128)}, u32[]{:S(2)}) %copy-start.1) | copy-done | bytes 196632
  2.8 0.0 copy-start.2
  2.8 0.7 copy-done.2
  3.5 0.0 copy-start.3
  3.5 0.7 copy-done.3
  4.2 72.5 %shard_map.46 = f32[192,256]{1,0:T(8,128)S(1)} custom-call(f32[2,192,2048]{2,1,0:T(8,128)S(1)} %bitcast.4, f32[192,256]{1,0:T(8,128)S(1)} %bitcast.6, f32[1,2048]{1,0:T(1,128)S(1)} %bitcast.7, f32[2]{0:T(128)S(1)} %copy-done.3), custom_call_target="tpu_custom_call" | custom-call | tf_op jit(solution)/shard_map/pallas_call | solution.py:554
  76.7 0.7 copy.6
Async XLA Ops:
  0.0 1.9 %copy-start = (f32[2,2048,192]{1,2,0:T(8,128)S(1)}, f32[2,2048,192]{1,2,0:T(8,128)}, u32[]{:S(2)}) copy-start(f32[2,2048,192]{1,2,0:T(8,128)} %param.4) | copy-start | bytes 9437188
  1.9 0.9 %copy-start.1 = (f32[256,192]{0,1:T(8,128)S(1)}, f32[256,192]{0,1:T(8,128)}, u32[]{:S(2)}) copy-start(f32[256,192]{0,1:T(8,128)} %param.5) | copy-start | bytes 589828
  2.8 0.7 copy-start.2
  3.5 0.7 copy-start.3

commit v3 on v2

--- a/solution.py
+++ b/solution.py
@@ -176,8 +176,9 @@
     zl,
     gram,
     curv,
-    c_own,
-    c_in,
+    c_x,
+    c_part,
+    c_z,
     c_all,
     g_own,
     g_x,
@@ -225,17 +226,8 @@
 
     partner, right, left = slot(0, True), slot(1), slot(-1)
 
-    def other_cell(d):
-        return lax.rem(cell + d, cells)
-
     def other_samp(d):
         return lax.rem(samp + d, samps)
-
-    barrier = pltpu.get_barrier_semaphore()
-    for d in range(1, samps):
-        pl.semaphore_signal(barrier, inc=1, device_id={"samp": other_samp(d)}, device_id_type=MESH)
-    for d in range(1, cells):
-        pl.semaphore_signal(barrier, inc=1, device_id={"cell": other_cell(d)}, device_id_type=MESH)
 
     def columns(j):
         return pl.ds(pl.multiple_of(j * block, block), block)
@@ -251,6 +243,24 @@
     ]
     for load in loads:
         load.start()
+
+    barrier = pltpu.get_barrier_semaphore()
+
+    def along_x(d):
+        return lax.rem(x + d, lines) * line + z
+
+    def along_z(d):
+        return x * line + lax.rem(z + d, line)
+
+    for friend in (right, left, partner):
+        pl.semaphore_signal(barrier, inc=1, device_id={"samp": friend}, device_id_type=MESH)
+    for d in range(1, line):
+        pl.semaphore_signal(barrier, inc=1, device_id={"cell": along_z(d)}, device_id_type=MESH)
+    for d in range(1, lines):
+        pl.semaphore_signal(barrier, inc=1, device_id={"cell": along_x(d)}, device_id_type=MESH)
+    for friend in (slot(2), slot(1, True), slot(2, True), slot(-1, True)):
+        pl.semaphore_signal(barrier, inc=1, device_id={"samp": friend}, device_id_type=MESH)
+
     for j in range(samps):
         load_bases(j).start()
 
@@ -260,6 +270,133 @@
     for load in loads:
         load.wait()
     mine = gathered.at[samp]
+    pl.semaphore_wait(barrier, lines + line + samps - 3)
+
+    def remote(src, dst, send_sem, recv_sem, **to):
+        copy = pltpu.make_async_remote_copy(
+            src_ref=src, dst_ref=dst, send_sem=send_sem, recv_sem=recv_sem, device_id=to, device_id_type=MESH
+        )
+        copy.start()
+        return copy
+
+    def send(src, dst, send_sem, recv_sem, to):
+        return remote(src, dst, send_sem, recv_sem, samp=to)
+
+    def arrived(ref, sem):
+        pltpu.make_async_copy(ref, ref, sem).wait()
+
+    def rows(h):
+        return pl.ds(half * h, half)
+
+    sent = []
+    for h in (0, 1):
+        sent.append(send(mine.at[rows(h)], mine.at[rows(h)], gather_send.at[h], gather_left.at[h], right))
+        sent.append(send(mine.at[rows(1 - h)], mine.at[rows(1 - h)], gather_send.at[3 - h], gather_right.at[1 - h], left))
+    sent.append(send(mine, mine, gather_send.at[4], gather_pair.at[0], partner))
+
+    quarter = size // lines
+    owners = quarter // 8
+
+    class Reduction:
+        def __init__(self, own, x_in, part, z_in, whole, sem, shift):
+            self.own, self.x_in, self.part, self.z_in, self.whole = own, x_in, part, z_in, whole
+            self.sent = [reduce_send.at[sem + i] for i in range(4)]
+            self.recv = [reduce_recv.at[sem + i] for i in range(4)]
+            self.shift = shift
+            self.owns = self.is_owner(z)
+
+        def is_owner(self, z_of):
+            return (z_of >= self.shift) & (z_of < self.shift + owners)
+
+        def rows(self, x_of, z_of=None):
+            if z_of is None:
+                return pl.ds(pl.multiple_of(quarter * x_of, 8), quarter)
+            return pl.ds(pl.multiple_of(quarter * x_of + 8 * (z_of - self.shift), 8), 8)
+
+        def small(self, z_of):
+            return pl.ds(pl.multiple_of(8 * (z_of - self.shift), 8), 8)
+
+        def count(self, n):
+            return self.own.at[pl.ds(0, n)]
+
+        def counted(self, owner, rest, sem):
+            @pl.when(self.owns)
+            def _():
+                arrived(self.count(owner), sem)
+
+            if rest:
+
+                @pl.when(jnp.logical_not(self.owns))
+                def _():
+                    arrived(self.count(rest), sem)
+
+        def scatter_x(self):
+            for d in (2, 1, 3):
+                to = lax.rem(x + d, lines)
+                remote(self.own.at[self.rows(to)], self.x_in.at[x], self.sent[0], self.recv[0], cell=to * line + z)
+
+        def scatter_z(self):
+            self.x_in[x] = self.own[self.rows(x), :]
+            arrived(self.count(quarter * (lines - 1)), self.recv[0])
+            self.part[...] = jnp.sum(self.x_in[...], axis=0)
+            for d in (4, 3, 5, 2, 6, 1, 7):
+                to = lax.rem(z + d, line)
+
+                @pl.when(self.is_owner(to))
+                def _(to=to):
+                    src = self.part.at[self.small(to)]
+                    remote(src, self.z_in.at[z], self.sent[1], self.recv[1], cell=x * line + to)
+
+        def total(self):
+            self.z_in[z] = self.part[self.small(z), :]
+            arrived(self.count(8 * (line - 1)), self.recv[1])
+            return jnp.sum(self.z_in[...], axis=0)
+
+        def share_z(self):
+            piece = self.whole.at[self.rows(x, z)]
+            for d in (4, 3, 5, 2, 6, 1, 7):
+                remote(piece, piece, self.sent[2], self.recv[2], cell=along_z(d))
+
+        def share_x(self):
+            self.counted(quarter - 8, quarter, self.recv[2])
+            piece = self.whole.at[self.rows(x)]
+            for d in (2, 1, 3):
+                remote(piece, piece, self.sent[3], self.recv[3], cell=along_x(d))
+
+        def finish(self):
+            arrived(self.count(quarter * (lines - 1)), self.recv[3])
+
+        def drain(self):
+            arrived(self.count(quarter * (lines - 1)), self.sent[0])
+            self.counted(quarter - 8, quarter, self.sent[1])
+            self.counted(8 * (line - 1), 0, self.sent[2])
+            arrived(self.count(quarter * (lines - 1)), self.sent[3])
+
+    sum_c = Reduction(gram, c_x, c_part, c_z, c_all, 0, 0)
+    sum_g = Reduction(g_own, g_x, g_part, g_z, g_all, 4, line - owners)
+
+    def spread_h():
+        @pl.when(sum_g.owns)
+        def _():
+            total = sum_g.total()
+            g_all[sum_g.rows(x, z), : 2 * size] = total[:, : 2 * size]
+            h_in[samp] = total[:, 2 * size :]
+            for d in range(1, samps):
+                remote(h_in.at[samp], h_in.at[samp], reduce_send.at[8], reduce_recv.at[8], samp=other_samp(d))
+
+    def share_g():
+        @pl.when(sum_g.owns)
+        def _():
+            arrived(h_in.at[pl.ds(0, samps - 1)], reduce_recv.at[8])
+            g_all[sum_g.rows(x, z), 2 * size :] = jnp.sum(h_in[...], axis=0)
+            sum_g.share_z()
+
+    def share_c():
+        @pl.when(sum_c.owns)
+        def _():
+            c_all[sum_c.rows(x, z), :] = sum_c.total()
+            sum_c.share_z()
+
     reference = mine[...]
     g_own[:, 2 * size :] = dot3(split(reference), split(reference * weights(samp)), NT)
 
@@ -275,9 +412,6 @@
             curv[s] += dot3((high, low), split(value * mass), NT)
         return carry
 
-    curv[...] = jnp.zeros_like(curv)
-    lax.fori_loop(0, samps, own_gram, 0)
-    g_own[:, : 2 * size] = pack(curv[0], curv[1])
 
     def cross(j, first=False):
         value = gathered[j]
@@ -285,216 +419,64 @@
         zh[j, pl.ds(0, size), :] = high
         zl[j, pl.ds(0, size), :] = low
         at = pl.ds(size, 2 * size)
-        term = dot3((zh[j, at, :], zl[j, at, :]), split(value * weights(j)), NT)
+        term = dot3(split(value * weights(j)), (zh[j, at, :], zl[j, at, :]), NT)
         if first:
             gram[...] = term
         else:
             gram[...] += term
 
-    cross(samp, True)
-
-    pl.semaphore_wait(barrier, cells + samps - 2)
-
-    def remote(src, dst, send_sem, recv_sem, **to):
-        copy = pltpu.make_async_remote_copy(
-            src_ref=src, dst_ref=dst, send_sem=send_sem, recv_sem=recv_sem, device_id=to, device_id_type=MESH
-        )
-        copy.start()
-        return copy
-
-    def send(src, dst, send_sem, recv_sem, to):
-        return remote(src, dst, send_sem, recv_sem, samp=to)
-
-    def arrived(ref, sem):
-        pltpu.make_async_copy(ref, ref, sem).wait()
-
-    def rows(h):
-        return pl.ds(half * h, half)
-
-    sent = []
-    for h in (0, 1):
-        sent.append(send(mine.at[rows(h)], mine.at[rows(h)], gather_send.at[h], gather_left.at[h], right))
-        sent.append(send(mine.at[rows(1 - h)], mine.at[rows(1 - h)], gather_send.at[3 - h], gather_right.at[1 - h], left))
-    sent.append(send(mine, mine, gather_send.at[4], gather_pair.at[0], partner))
-
-    quarter = size // lines
-    owns_g = z < quarter // 8
-
-    def g_rows(x_of, z_of=None):
-        if z_of is None:
-            return pl.ds(pl.multiple_of(quarter * x_of, 8), quarter)
-        return pl.ds(pl.multiple_of(quarter * x_of + 8 * z_of, 8), 8)
-
-    def count_rows(n):
-        return g_own.at[pl.ds(0, n)]
-
-    def g_scatter_x():
-        for d in range(1, lines):
-            to = lax.rem(x + d, lines)
-            remote(g_own.at[g_rows(to)], g_x.at[x], reduce_send.at[0], reduce_recv.at[0], cell=to * line + z)
-
-    def g_scatter_z():
-        g_x[x] = g_own[g_rows(x), :]
-        arrived(count_rows(quarter * (lines - 1)), reduce_recv.at[0])
-        g_part[...] = jnp.sum(g_x[...], axis=0)
-        for d in range(1, line):
-            to = lax.rem(z + d, line)
-
-            @pl.when(to < quarter // 8)
-            def _(to=to):
-                src = g_part.at[pl.ds(pl.multiple_of(8 * to, 8), 8)]
-                remote(src, g_z.at[z], reduce_send.at[1], reduce_recv.at[1], cell=x * line + to)
-
-    def g_scatter_samp():
-        @pl.when(owns_g)
-        def _():
-            g_z[z] = g_part[pl.ds(pl.multiple_of(8 * z, 8), 8), :]
-            arrived(count_rows(8 * (line - 1)), reduce_recv.at[1])
-            total = jnp.sum(g_z[...], axis=0)
-            g_all[g_rows(x, z), : 2 * size] = total[:, : 2 * size]
-            h_in[samp] = total[:, 2 * size :]
-            for d in range(1, samps):
-                remote(h_in.at[samp], h_in.at[samp], reduce_send.at[2], reduce_recv.at[2], samp=other_samp(d))
-
-    def g_share_z():
-        @pl.when(owns_g)
-        def _():
-            arrived(h_in.at[pl.ds(0, samps - 1)], reduce_recv.at[2])
-            g_all[g_rows(x, z), 2 * size :] = jnp.sum(h_in[...], axis=0)
-            piece = g_all.at[g_rows(x, z)]
-            for d in range(1, line):
-                to = lax.rem(z + d, line)
-                remote(piece, piece, reduce_send.at[3], reduce_recv.at[3], cell=x * line + to)
-
-    def g_counted(owner, rest, sem):
-        @pl.when(owns_g)
-        def _():
-            arrived(count_rows(owner), sem)
-
-        if rest:
-
-            @pl.when(jnp.logical_not(owns_g))
-            def _():
-                arrived(count_rows(rest), sem)
-
-    def g_share_x():
-        g_counted(quarter - 8, quarter, reduce_recv.at[3])
-        piece = g_all.at[g_rows(x)]
-        for d in range(1, lines):
-            to = lax.rem(x + d, lines)
-            remote(piece, piece, reduce_send.at[4], reduce_recv.at[4], cell=to * line + z)
-
-    def g_finish():
-        arrived(count_rows(quarter * (lines - 1)), reduce_recv.at[4])
-
-    def g_drain():
-        arrived(count_rows(quarter * (lines - 1)), reduce_send.at[0])
-        g_counted(quarter - 8, quarter, reduce_send.at[1])
-
-        @pl.when(owns_g)
-        def _():
-            arrived(h_in.at[pl.ds(0, samps - 1)], reduce_send.at[2])
-
-        g_counted(8 * (line - 1), 0, reduce_send.at[3])
-        arrived(count_rows(quarter * (lines - 1)), reduce_send.at[4])
-
-    group = 16
-    per_line = size // group // lines
-    z_pair = z // 2
-    owns_c = (lax.rem(z, 2) == lax.rem(x + core, 2)) & (z_pair < per_line)
-
-    def c_rows(x_of, pair_of):
-        return pl.ds(pl.multiple_of(group * (per_line * x_of + pair_of), group), group)
-
-    def c_scatter():
-        for dx in range(lines):
-            to_x = lax.rem(x + dx, lines)
-            for dq in range(per_line):
-                to_pair = lax.rem(z_pair + dq, per_line)
-                to = to_x * line + 2 * to_pair + lax.rem(to_x + core, 2)
-
-                def one(to=to, to_x=to_x, to_pair=to_pair):
-                    src = c_own.at[c_rows(to_x, to_pair)]
-                    remote(src, c_in.at[cell], reduce_send.at[5], reduce_recv.at[5], cell=to)
-
-                if dx:
-                    one()
-                else:
-                    pl.when(to != cell)(one)
-
-    def c_share():
-        @pl.when(owns_c)
-        def _():
-            here = c_rows(x, z_pair)
-            c_in[cell] = c_own[here, :]
-            arrived(c_in.at[pl.ds(0, cells - 1)], reduce_recv.at[5])
-            c_all[here, :] = jnp.sum(c_in[...], axis=0)
-            for d in range(1, cells):
-                remote(c_all.at[here], c_all.at[here], reduce_send.at[6], reduce_recv.at[6], cell=other_cell(d))
-
-    def c_counted(sem):
-        @pl.when(owns_c)
-        def _():
-            arrived(c_own.at[pl.ds(0, size - group)], sem)
-
-        @pl.when(jnp.logical_not(owns_c))
-        def _():
-            arrived(c_own, sem)
-
-    def c_drain():
-        c_counted(reduce_send.at[5])
-
-        @pl.when(owns_c)
-        def _():
-            arrived(c_in.at[pl.ds(0, cells - 1)], reduce_send.at[6])
-
-    g_scatter_x()
+    curv[...] = jnp.zeros_like(curv)
+    lax.fori_loop(0, samps // 2, own_gram, 0)
+    from_left, from_right, far = gathered.at[left], gathered.at[right], gathered.at[slot(2)]
     arrived(mine.at[rows(0)], gather_left.at[0])
-    from_left, from_right, far = gathered.at[left], gathered.at[right], gathered.at[slot(2)]
     sent.append(send(from_left.at[rows(0)], from_left.at[rows(0)], gather_send.at[5], gather_far.at[0], right))
     arrived(mine.at[rows(1)], gather_right.at[1])
     sent.append(send(from_right.at[rows(1)], from_right.at[rows(1)], gather_send.at[6], gather_far.at[1], left))
+    lax.fori_loop(samps // 2, samps, own_gram, 0)
+    g_own[:, : 2 * size] = pack(curv[0], curv[1])
+    sum_g.scatter_x()
     arrived(mine.at[rows(1)], gather_left.at[1])
     sent.append(send(from_left, from_left, gather_send.at[7], gather_pair.at[1], partner))
     arrived(mine.at[rows(0)], gather_right.at[0])
     sent.append(send(from_right, from_right, gather_send.at[8], gather_pair.at[2], partner))
     arrived(mine, gather_pair.at[0])
+    cross(samp, True)
     cross(partner)
     cross(left)
     cross(right)
-    g_scatter_z()
     arrived(mine.at[rows(0)], gather_far.at[0])
     arrived(mine.at[rows(1)], gather_far.at[1])
     sent.append(send(far, far, gather_send.at[9], gather_pair.at[3], partner))
+    sum_g.scatter_z()
     cross(slot(2))
     for i, step in ((1, -1), (2, 1), (3, 2)):
         arrived(mine, gather_pair.at[i])
         cross(slot(step, True))
 
-    c_own[...] = pack(gram[:size], gram[size:])
-    c_scatter()
-    g_scatter_samp()
-    c_share()
-    g_share_z()
-    c_counted(reduce_recv.at[6])
-
-    cross_t = unpack(c_all[...])
-    normal = [exact(c, c, NT) for c in cross_t]
-    minus_inverse = invert(normal, leaf, g_share_x)
-    inverses = [-exact(m, c) for m, c in zip(minus_inverse, cross_t)]
-
-    g_finish()
+    sum_c.scatter_x()
+    spread_h()
+    sum_c.scatter_z()
+    share_c()
+    sum_c.share_x()
+    share_g()
+    sum_c.finish()
+
+    cross_gram = [c_all[:, :size], c_all[:, size:]]
+    normal = [exact(c, c, NT) for c in cross_gram]
+    minus_inverse = invert(normal, leaf, sum_g.share_x)
+    turned = [-exact(m, c) for m, c in zip(minus_inverse, cross_gram)]
+
+    sum_g.finish()
     of_bases = unpack(g_all[:, : 2 * size])
     of_reference = g_all[:, 2 * size :]
     plain = jnp.zeros((size, size), F32)
     for s in range(2):
-        inverse = split(inverses[s])
-        turned = inverses[s].T
-        middle = dot3(split(of_bases[s]), inverse) - 2.0 * cross_t[s]
-        curvature = matmul(turned, middle) + of_reference
+        pieces = split(turned[s])
+        middle = dot3(split(of_bases[s]), pieces, NT)
+        curvature = dot3(pieces, split(middle)) - 2.0 * dot3(pieces, split(cross_gram[s]), NT) + of_reference
         factors = series(curvature) * weight_ref[s]
         plain = plain - factors
-        lhs_h[s + 1], lhs_l[s + 1] = split(matmul(factors, turned))
+        lhs_h[s + 1], lhs_l[s + 1] = split(dot3(split(factors), pieces))
     lhs_h[0], lhs_l[0] = split(plain)
 
     def term(j):
@@ -538,8 +520,12 @@
 
     for copy in sent:
         copy.wait_send()
-    c_drain()
-    g_drain()
+    sum_c.drain()
+    sum_g.drain()
+
+    @pl.when(sum_g.owns)
+    def _():
+        arrived(h_in.at[pl.ds(0, samps - 1)], reduce_send.at[8])
 
 
 def body(bases, reference_basis, mass, interp_weights):
@@ -549,7 +535,7 @@
     packed, wide = 2 * size, 3 * size
     half = size // 2
     hbm, vmem = pl.BlockSpec(memory_space=pltpu.HBM), pl.BlockSpec(memory_space=pltpu.VMEM)
-    line, group = 8, 16
+    line = 8
     lines = cells // line
     result = pl.pallas_call(
         functools.partial(kernel, cells, depth * cells, samps),
@@ -563,10 +549,11 @@
             pltpu.VMEM((samps, size, block), F32),
             pltpu.VMEM((samps, 3 * size, block), BF16),
             pltpu.VMEM((samps, 3 * size, block), BF16),
-            pltpu.VMEM((packed, size), F32),
+            pltpu.VMEM((size, packed), F32),
             pltpu.VMEM((2, size, size), F32),
-            pltpu.VMEM((size, packed), F32),
-            pltpu.VMEM((cells, group, packed), F32),
+            pltpu.VMEM((lines, size // lines, packed), F32),
+            pltpu.VMEM((size // lines, packed), F32),
+            pltpu.VMEM((line, 8, packed), F32),
             pltpu.VMEM((size, packed), F32),
             pltpu.VMEM((size, wide), F32),
             pltpu.VMEM((lines, size // lines, wide), F32),
@@ -588,8 +575,8 @@
             pltpu.SemaphoreType.DMA((2,)),
             pltpu.SemaphoreType.DMA((2,)),
             pltpu.SemaphoreType.DMA((4,)),
-            pltpu.SemaphoreType.DMA((7,)),
-            pltpu.SemaphoreType.DMA((7,)),
+            pltpu.SemaphoreType.DMA((9,)),
+            pltpu.SemaphoreType.DMA((9,)),
             pltpu.SemaphoreType.DMA((10,)),
             pltpu.SemaphoreType.DMA((4,)),
             pltpu.SemaphoreType.DMA((2,)),

time: 77.5 us -> 72.8 us (0.939)
  the two profiles are of different devices: /device:TPU:8 before, /device:TPU:6 now
where the time goes in v3:
time: 72.8 us; the launch traced here: 72.6 us
  Pallas kernels  67.7 us (93%)
  local copies, waits for them, and re-layouts  4.85 us (7%)
    pallas_call x1, Pallas kernels, body(): pl.pallas_call(functools.partial(kernel, cells, depth * cells, samps), ou...  67.7 us
    unnamed x9, local copies, waits for them, and re-layouts  4.85 us

profile of v3, /device:TPU:6, one launch (start us, length us, event | category | flops | bytes accessed | tf_op | source)
XLA Modules:
  0.0 72.6 jit_solution(8114296454635974344)
XLA Ops:
  0.0 0.0 copy-start
  0.0 1.9 %copy-done = f32[2,2048,192]{1,2,0:T(8,128)S(1)} copy-done((f32[2,2048,192]{1,2,0:T(8,128)S(1)}, f32[2,2048,192]{1,2,0:T(8,128)}, u32[]{:S(2)}) %copy-start) | copy-done | bytes 3145752
  1.9 0.0 copy-start.1
  1.9 0.9 %copy-done.1 = f32[256,192]{0,1:T(8,128)S(1)} copy-done((f32[256,192]{0,1:T(8,128)S(1)}, f32[256,192]{0,1:T(8,128)}, u32[]{:S(2)}) %copy-start.1) | copy-done | bytes 196632
  2.8 0.0 copy-start.2
  2.8 0.7 copy-done.2
  3.5 0.0 copy-start.3
  3.5 0.7 copy-done.3
  4.2 67.7 %shard_map.46 = f32[192,256]{1,0:T(8,128)S(1)} custom-call(f32[2,192,2048]{2,1,0:T(8,128)S(1)} %bitcast.4, f32[192,256]{1,0:T(8,128)S(1)} %bitcast.6, f32[1,2048]{1,0:T(1,128)S(1)} %bitcast.7, f32[2]{0:T(128)S(1)} %copy-done.3), custom_call_target="tpu_custom_call" | custom-call | tf_op jit(solution)/shard_map/pallas_call | solution.py:540
  71.9 0.7 copy.6
Async XLA Ops:
  0.0 1.9 %copy-start = (f32[2,2048,192]{1,2,0:T(8,128)S(1)}, f32[2,2048,192]{1,2,0:T(8,128)}, u32[]{:S(2)}) copy-start(f32[2,2048,192]{1,2,0:T(8,128)} %param.4) | copy-start | bytes 9437188
  1.9 0.9 %copy-start.1 = (f32[256,192]{0,1:T(8,128)S(1)}, f32[256,192]{0,1:T(8,128)}, u32[]{:S(2)}) copy-start(f32[256,192]{0,1:T(8,128)} %param.5) | copy-start | bytes 589828
  2.8 0.7 copy-start.2
  3.5 0.7 copy-start.3

commit v4 on v3

--- a/solution.py
+++ b/solution.py
@@ -129,34 +129,35 @@
         if i == 0:
             between()
         minus_inverse = leaf_ref[...]
+        inside = (lane >= LEAF * i) & (lane < LEAF * (i + 1))
+        panels = [jnp.where(lane == row + LEAF * i, 1.0, jnp.where(inside, 0.0, -n[own, :])) for n in normal]
+        scaled = [exact(minus_inverse[:, LEAF * s : LEAF * (s + 1)], panels[s]) for s in range(2)]
+        cleared = (every_lane >= LEAF * i) & (every_lane < LEAF * (i + 1))
+        products = [exact(n[:, own], r) for n, r in zip(normal, scaled)]
         updated = []
-        for s, n in enumerate(normal):
-            panel = jnp.where(
-                lane == row + LEAF * i, 1.0, jnp.where((lane >= LEAF * i) & (lane < LEAF * (i + 1)), 0.0, -n[own, :])
-            )
-            scaled = exact(minus_inverse[:, LEAF * s : LEAF * (s + 1)], panel)
-            kept = jnp.where((every_lane >= LEAF * i) & (every_lane < LEAF * (i + 1)), 0.0, n)
-            new = kept - exact(n[:, own], scaled)
-            parts = [new[: LEAF * i], scaled, new[LEAF * (i + 1) :]]
+        for n, r, product in zip(normal, scaled, products):
+            new = jnp.where(cleared, 0.0, n) - product
+            parts = [new[: LEAF * i], r, new[LEAF * (i + 1) :]]
             updated.append(jnp.concatenate([part for part in parts if part.shape[0]], axis=0))
         normal = updated
     return normal
 
 
-def series(curvature):
-    size = curvature.shape[0]
+def series(curvatures):
+    size = curvatures[0].shape[0]
     diagonal = lax.broadcasted_iota(jnp.int32, (size, size), 0) == lax.broadcasted_iota(jnp.int32, (size, size), 1)
     weight = [(-1.0) ** n / (2 * n + 1) for n in range(NTERMS)]
 
-    def pair(n):
+    def pair(curvature, n):
         return weight[n + 1] * curvature + jnp.where(diagonal, weight[n], 0.0)
 
-    pieces = split(curvature)
-    square = split(dot3(pieces, pieces))
-    result = pair(NTERMS - 2)
+    pieces = [split(c) for c in curvatures]
+    squares = [split(dot3(p, p)) for p in pieces]
+    results = [pair(c, NTERMS - 2) for c in curvatures]
     for n in range(NTERMS - 4, -1, -2):
-        result = pair(n) + dot3(square, split(result))
-    return result
+        products = [dot3(square, split(r)) for square, r in zip(squares, results)]
+        results = [pair(c, n) + product for c, product in zip(curvatures, products)]
+    return results
 
 
 def kernel(
@@ -184,6 +185,7 @@
     g_x,
     g_part,
     g_z,
+    h_pair,
     h_in,
     g_all,
     leaf,
@@ -226,20 +228,17 @@
 
     partner, right, left = slot(0, True), slot(1), slot(-1)
 
-    def other_samp(d):
-        return lax.rem(samp + d, samps)
-
     def columns(j):
         return pl.ds(pl.multiple_of(j * block, block), block)
 
-    def load_bases(j):
-        at = bases.at[:, :, columns(j)]
-        return pltpu.make_async_copy(bases_hbm.at[:, :, columns(j)], at, load_sem.at[j])
+    def load_bases(h):
+        at = pl.ds(h * block * (samps // 2), block * (samps // 2))
+        return pltpu.make_async_copy(bases_hbm.at[:, :, at], bases.at[:, :, at], load_sem.at[h])
 
     loads = [
-        pltpu.make_async_copy(mass_hbm, mass_row, load_sem.at[samps]),
-        pltpu.make_async_copy(own_hbm, gathered.at[samp], load_sem.at[samps + 1]),
-        pltpu.make_async_copy(weight_hbm, weight_ref, load_sem.at[samps + 2]),
+        pltpu.make_async_copy(mass_hbm, mass_row, load_sem.at[2]),
+        pltpu.make_async_copy(own_hbm, gathered.at[samp], load_sem.at[3]),
+        pltpu.make_async_copy(weight_hbm, weight_ref, load_sem.at[4]),
     ]
     for load in loads:
         load.start()
@@ -252,17 +251,12 @@
     def along_z(d):
         return x * line + lax.rem(z + d, line)
 
-    for friend in (right, left, partner):
+    for friend in (right, left, partner, slot(2)):
         pl.semaphore_signal(barrier, inc=1, device_id={"samp": friend}, device_id_type=MESH)
     for d in range(1, line):
         pl.semaphore_signal(barrier, inc=1, device_id={"cell": along_z(d)}, device_id_type=MESH)
     for d in range(1, lines):
         pl.semaphore_signal(barrier, inc=1, device_id={"cell": along_x(d)}, device_id_type=MESH)
-    for friend in (slot(2), slot(1, True), slot(2, True), slot(-1, True)):
-        pl.semaphore_signal(barrier, inc=1, device_id={"samp": friend}, device_id_type=MESH)
-
-    for j in range(samps):
-        load_bases(j).start()
 
     def weights(j):
         return mass_row[:, columns(j)] * (1.0 / depth)
@@ -270,7 +264,7 @@
     for load in loads:
         load.wait()
     mine = gathered.at[samp]
-    pl.semaphore_wait(barrier, lines + line + samps - 3)
+    pl.semaphore_wait(barrier, lines + line + chips - 2)
 
     def remote(src, dst, send_sem, recv_sem, **to):
         copy = pltpu.make_async_remote_copy(
@@ -293,6 +287,9 @@
         sent.append(send(mine.at[rows(h)], mine.at[rows(h)], gather_send.at[h], gather_left.at[h], right))
         sent.append(send(mine.at[rows(1 - h)], mine.at[rows(1 - h)], gather_send.at[3 - h], gather_right.at[1 - h], left))
     sent.append(send(mine, mine, gather_send.at[4], gather_pair.at[0], partner))
+
+    for h in (0, 1):
+        load_bases(h).start()
 
     quarter = size // lines
     owners = quarter // 8
@@ -380,14 +377,21 @@
         def _():
             total = sum_g.total()
             g_all[sum_g.rows(x, z), : 2 * size] = total[:, : 2 * size]
-            h_in[samp] = total[:, 2 * size :]
-            for d in range(1, samps):
-                remote(h_in.at[samp], h_in.at[samp], reduce_send.at[8], reduce_recv.at[8], samp=other_samp(d))
+            h_pair[0] = total[:, 2 * size :]
+            remote(h_pair.at[0], h_pair.at[1], reduce_send.at[8], reduce_recv.at[8], samp=partner)
+
+    def spread_pair():
+        @pl.when(sum_g.owns)
+        def _():
+            arrived(h_pair.at[0], reduce_recv.at[8])
+            h_in[y] = h_pair[0] + h_pair[1]
+            for step in (2, 1, -1):
+                remote(h_in.at[y], h_in.at[y], reduce_send.at[9], reduce_recv.at[9], samp=slot(step))
 
     def share_g():
         @pl.when(sum_g.owns)
         def _():
-            arrived(h_in.at[pl.ds(0, samps - 1)], reduce_recv.at[8])
+            arrived(h_in.at[pl.ds(0, chips - 1)], reduce_recv.at[9])
             g_all[sum_g.rows(x, z), 2 * size :] = jnp.sum(h_in[...], axis=0)
             sum_g.share_z()
 
@@ -401,7 +405,6 @@
     g_own[:, 2 * size :] = dot3(split(reference), split(reference * weights(samp)), NT)
 
     def own_gram(j, carry):
-        load_bases(j).wait()
         mass = weights(j)
         for s in range(2):
             value = bases[s, :, columns(j)]
@@ -426,12 +429,14 @@
             gram[...] += term
 
     curv[...] = jnp.zeros_like(curv)
+    load_bases(0).wait()
     lax.fori_loop(0, samps // 2, own_gram, 0)
     from_left, from_right, far = gathered.at[left], gathered.at[right], gathered.at[slot(2)]
     arrived(mine.at[rows(0)], gather_left.at[0])
     sent.append(send(from_left.at[rows(0)], from_left.at[rows(0)], gather_send.at[5], gather_far.at[0], right))
     arrived(mine.at[rows(1)], gather_right.at[1])
     sent.append(send(from_right.at[rows(1)], from_right.at[rows(1)], gather_send.at[6], gather_far.at[1], left))
+    load_bases(1).wait()
     lax.fori_loop(samps // 2, samps, own_gram, 0)
     g_own[:, : 2 * size] = pack(curv[0], curv[1])
     sum_g.scatter_x()
@@ -456,27 +461,31 @@
     sum_c.scatter_x()
     spread_h()
     sum_c.scatter_z()
+    spread_pair()
     share_c()
     sum_c.share_x()
     share_g()
     sum_c.finish()
+    sum_g.share_x()
 
     cross_gram = [c_all[:, :size], c_all[:, size:]]
     normal = [exact(c, c, NT) for c in cross_gram]
-    minus_inverse = invert(normal, leaf, sum_g.share_x)
+    minus_inverse = invert(normal, leaf, lambda: None)
     turned = [-exact(m, c) for m, c in zip(minus_inverse, cross_gram)]
 
     sum_g.finish()
     of_bases = unpack(g_all[:, : 2 * size])
     of_reference = g_all[:, 2 * size :]
-    plain = jnp.zeros((size, size), F32)
+    pieces = [split(t) for t in turned]
+    middles = [dot3(split(g), p, NT) for g, p in zip(of_bases, pieces)]
+    mixed = [dot3(p, split(c), NT) for p, c in zip(pieces, cross_gram)]
+    outer = [dot3(p, split(m)) for p, m in zip(pieces, middles)]
+    results = series([o - 2.0 * m + of_reference for o, m in zip(outer, mixed)])
+    factors = [f * weight_ref[s] for s, f in enumerate(results)]
+    plain = -(factors[0] + factors[1])
+    finals = [dot3(split(f), p) for f, p in zip(factors, pieces)]
     for s in range(2):
-        pieces = split(turned[s])
-        middle = dot3(split(of_bases[s]), pieces, NT)
-        curvature = dot3(pieces, split(middle)) - 2.0 * dot3(pieces, split(cross_gram[s]), NT) + of_reference
-        factors = series(curvature) * weight_ref[s]
-        plain = plain - factors
-        lhs_h[s + 1], lhs_l[s + 1] = split(dot3(split(factors), pieces))
+        lhs_h[s + 1], lhs_l[s + 1] = split(finals[s])
     lhs_h[0], lhs_l[0] = split(plain)
 
     def term(j):
@@ -525,7 +534,8 @@
 
     @pl.when(sum_g.owns)
     def _():
-        arrived(h_in.at[pl.ds(0, samps - 1)], reduce_send.at[8])
+        arrived(h_pair.at[0], reduce_send.at[8])
+        arrived(h_in.at[pl.ds(0, chips - 1)], reduce_send.at[9])
 
 
 def body(bases, reference_basis, mass, interp_weights):
@@ -559,7 +569,8 @@
             pltpu.VMEM((lines, size // lines, wide), F32),
             pltpu.VMEM((size // lines, wide), F32),
             pltpu.VMEM((line, 8, wide), F32),
-            pltpu.VMEM((samps, 8, size), F32),
+            pltpu.VMEM((2, 8, size), F32),
+            pltpu.VMEM((samps // 2, 8, size), F32),
             pltpu.VMEM((size, wide), F32),
             pltpu.VMEM((LEAF, 2 * LEAF), F32),
             pltpu.VMEM((3, size, size), BF16),
@@ -569,14 +580,14 @@
             pltpu.VMEM((3, size, block), F32),
             pltpu.VMEM((2, half, block), F32),
             pltpu.VMEM((2, size, block), F32),
-            pltpu.SemaphoreType.DMA((samps + 3,)),
+            pltpu.SemaphoreType.DMA((5,)),
             pltpu.SemaphoreType.DMA((10,)),
             pltpu.SemaphoreType.DMA((2,)),
             pltpu.SemaphoreType.DMA((2,)),
             pltpu.SemaphoreType.DMA((2,)),
             pltpu.SemaphoreType.DMA((4,)),
-            pltpu.SemaphoreType.DMA((9,)),
-            pltpu.SemaphoreType.DMA((9,)),
+            pltpu.SemaphoreType.DMA((10,)),
+            pltpu.SemaphoreType.DMA((10,)),
             pltpu.SemaphoreType.DMA((10,)),
             pltpu.SemaphoreType.DMA((4,)),
             pltpu.SemaphoreType.DMA((2,)),

time: 72.8 us -> 71.8 us (0.986)
  the two profiles are of different devices: /device:TPU:6 before, /device:TPU:8 now
where the time goes in v4:
time: 71.8 us; the launch traced here: 71.4 us
  Pallas kernels  66.5 us (93%)
  local copies, waits for them, and re-layouts  4.85 us (7%)
    pallas_call x1, Pallas kernels, body(): pl.pallas_call(functools.partial(kernel, cells, depth * cells, samps), ou...  66.5 us
    unnamed x9, local copies, waits for them, and re-layouts  4.85 us

profile of v4, /device:TPU:8, one launch (start us, length us, event | category | flops | bytes accessed | tf_op | source)
XLA Modules:
  0.0 71.4 jit_solution(3441944382946089381)
XLA Ops:
  0.0 0.0 copy-start
  0.0 1.9 %copy-done = f32[2,2048,192]{1,2,0:T(8,128)S(1)} copy-done((f32[2,2048,192]{1,2,0:T(8,128)S(1)}, f32[2,2048,192]{1,2,0:T(8,128)}, u32[]{:S(2)}) %copy-start) | copy-done | bytes 3145752
  1.9 0.0 copy-start.1
  1.9 0.9 %copy-done.1 = f32[256,192]{0,1:T(8,128)S(1)} copy-done((f32[256,192]{0,1:T(8,128)S(1)}, f32[256,192]{0,1:T(8,128)}, u32[]{:S(2)}) %copy-start.1) | copy-done | bytes 196632
  2.8 0.0 copy-start.2
  2.8 0.7 copy-done.2
  3.5 0.0 copy-start.3
  3.5 0.7 copy-done.3
  4.2 66.5 %shard_map.46 = f32[192,256]{1,0:T(8,128)S(1)} custom-call(f32[2,192,2048]{2,1,0:T(8,128)S(1)} %bitcast.4, f32[192,256]{1,0:T(8,128)S(1)} %bitcast.6, f32[1,2048]{1,0:T(1,128)S(1)} %bitcast.7, f32[2]{0:T(128)S(1)} %copy-done.3), custom_call_target="tpu_custom_call" | custom-call | tf_op jit(solution)/shard_map/pallas_call | solution.py:550
  70.7 0.7 copy.6
Async XLA Ops:
  0.0 1.9 %copy-start = (f32[2,2048,192]{1,2,0:T(8,128)S(1)}, f32[2,2048,192]{1,2,0:T(8,128)}, u32[]{:S(2)}) copy-start(f32[2,2048,192]{1,2,0:T(8,128)} %param.4) | copy-start | bytes 9437188
  1.9 0.9 %copy-start.1 = (f32[256,192]{0,1:T(8,128)S(1)}, f32[256,192]{0,1:T(8,128)}, u32[]{:S(2)}) copy-start(f32[256,192]{0,1:T(8,128)} %param.5) | copy-start | bytes 589828
  2.8 0.7 copy-start.2
  3.5 0.7 copy-start.3

commit v5 on v4

--- a/solution.py
+++ b/solution.py
@@ -452,25 +452,24 @@
     arrived(mine.at[rows(0)], gather_far.at[0])
     arrived(mine.at[rows(1)], gather_far.at[1])
     sent.append(send(far, far, gather_send.at[9], gather_pair.at[3], partner))
-    sum_g.scatter_z()
     cross(slot(2))
     for i, step in ((1, -1), (2, 1), (3, 2)):
         arrived(mine, gather_pair.at[i])
         cross(slot(step, True))
 
     sum_c.scatter_x()
+    sum_g.scatter_z()
+    sum_c.scatter_z()
     spread_h()
-    sum_c.scatter_z()
+    share_c()
     spread_pair()
-    share_c()
     sum_c.share_x()
     share_g()
     sum_c.finish()
-    sum_g.share_x()
 
     cross_gram = [c_all[:, :size], c_all[:, size:]]
     normal = [exact(c, c, NT) for c in cross_gram]
-    minus_inverse = invert(normal, leaf, lambda: None)
+    minus_inverse = invert(normal, leaf, sum_g.share_x)
     turned = [-exact(m, c) for m, c in zip(minus_inverse, cross_gram)]
 
     sum_g.finish()

time: 71.8 us -> 69 us (0.961)
  Pallas kernels: 66.5 us -> 64 us
    pallas_call x1, Pallas kernels: 66.5 us -> 64 us  [body(): pl.pallas_call(functools.partial(kernel, cells, depth * cells, samps), ou...]
where the time goes in v5:
time: 69 us; the launch traced here: 68.8 us
  Pallas kernels  64 us (93%)
  local copies, waits for them, and re-layouts  4.85 us (7%)
    pallas_call x1, Pallas kernels, body(): pl.pallas_call(functools.partial(kernel, cells, depth * cells, samps), ou...  64 us
    unnamed x9, local copies, waits for them, and re-layouts  4.85 us

profile of v5, /device:TPU:8, one launch (start us, length us, event | category | flops | bytes accessed | tf_op | source)
XLA Modules:
  0.0 68.8 jit_solution(8189538668521964183)
XLA Ops:
  0.0 0.0 copy-start
  0.0 1.9 %copy-done = f32[2,2048,192]{1,2,0:T(8,128)S(1)} copy-done((f32[2,2048,192]{1,2,0:T(8,128)S(1)}, f32[2,2048,192]{1,2,0:T(8,128)}, u32[]{:S(2)}) %copy-start) | copy-done | bytes 3145752
  1.9 0.0 copy-start.1
  1.9 0.9 %copy-done.1 = f32[256,192]{0,1:T(8,128)S(1)} copy-done((f32[256,192]{0,1:T(8,128)S(1)}, f32[256,192]{0,1:T(8,128)}, u32[]{:S(2)}) %copy-start.1) | copy-done | bytes 196632
  2.8 0.0 copy-start.2
  2.8 0.7 %copy-done.2 = f32[2048]{0:T(1024)S(1)} copy-done((f32[2048]{0:T(1024)S(1)}, f32[2048]{0:T(1024)}, u32[]{:S(2)}) %copy-start.2) | copy-done | bytes 8216
  3.5 0.0 copy-start.3
  3.5 0.7 copy-done.3
  4.2 64.0 %shard_map.46 = f32[192,256]{1,0:T(8,128)S(1)} custom-call(f32[2,192,2048]{2,1,0:T(8,128)S(1)} %bitcast.4, f32[192,256]{1,0:T(8,128)S(1)} %bitcast.6, f32[1,2048]{1,0:T(1,128)S(1)} %bitcast.7, f32[2]{0:T(128)S(1)} %copy-done.3), custom_call_target="tpu_custom_call" | custom-call | tf_op jit(solution)/shard_map/pallas_call | solution.py:549
  68.1 0.7 copy.6
Async XLA Ops:
  0.0 1.9 %copy-start = (f32[2,2048,192]{1,2,0:T(8,128)S(1)}, f32[2,2048,192]{1,2,0:T(8,128)}, u32[]{:S(2)}) copy-start(f32[2,2048,192]{1,2,0:T(8,128)} %param.4) | copy-start | bytes 9437188
  1.9 0.9 %copy-start.1 = (f32[256,192]{0,1:T(8,128)S(1)}, f32[256,192]{0,1:T(8,128)}, u32[]{:S(2)}) copy-start(f32[256,192]{0,1:T(8,128)} %param.5) | copy-start | bytes 589828
  2.8 0.7 %copy-start.2 = (f32[2048]{0:T(1024)S(1)}, f32[2048]{0:T(1024)}, u32[]{:S(2)}) copy-start(f32[2048]{0:T(1024)} %param.6) | copy-start | bytes 24580
  3.5 0.7 copy-start.3

commit v6 on v5

--- a/solution.py
+++ b/solution.py
@@ -117,30 +117,30 @@
     lax.fori_loop(0, LEAF // 8, step, 0)
 
 
-def invert(normal, leaf_ref, between):
+def solve(normal, right, leaf_ref, between):
     size = normal[0].shape[0]
-    row = lax.broadcasted_iota(jnp.int32, (LEAF, size), 0)
-    lane = lax.broadcasted_iota(jnp.int32, (LEAF, size), 1)
-    every_lane = lax.broadcasted_iota(jnp.int32, (size, size), 1)
+    pivots = [n[:, :LEAF] for n in normal]
+    rests = [jnp.concatenate([r, n[:, LEAF:]], axis=1) for n, r in zip(normal, right)]
     for i in range(size // LEAF):
         own = slice(LEAF * i, LEAF * (i + 1))
-        leaf_ref[...] = jnp.concatenate([n[own, own] for n in normal], axis=1)
+        leaf_ref[...] = jnp.concatenate([p[own] for p in pivots], axis=1)
         sweep_leaf(leaf_ref)
         if i == 0:
             between()
         minus_inverse = leaf_ref[...]
-        inside = (lane >= LEAF * i) & (lane < LEAF * (i + 1))
-        panels = [jnp.where(lane == row + LEAF * i, 1.0, jnp.where(inside, 0.0, -n[own, :])) for n in normal]
-        scaled = [exact(minus_inverse[:, LEAF * s : LEAF * (s + 1)], panels[s]) for s in range(2)]
-        cleared = (every_lane >= LEAF * i) & (every_lane < LEAF * (i + 1))
-        products = [exact(n[:, own], r) for n, r in zip(normal, scaled)]
+        minus_rows = [exact(minus_inverse[:, LEAF * s : LEAF * (s + 1)], rests[s][own]) for s in range(2)]
+        products = [exact(p, r) for p, r in zip(pivots, minus_rows)]
         updated = []
-        for n, r, product in zip(normal, scaled, products):
-            new = jnp.where(cleared, 0.0, n) - product
-            parts = [new[: LEAF * i], r, new[LEAF * (i + 1) :]]
+        for rest, rows, product in zip(rests, minus_rows, products):
+            new = rest + product
+            parts = [new[: LEAF * i], -rows, new[LEAF * (i + 1) :]]
             updated.append(jnp.concatenate([part for part in parts if part.shape[0]], axis=0))
-        normal = updated
-    return normal
+        pivots = [u[:, size : size + LEAF] for u in updated]
+        rests = [
+            jnp.concatenate([u[:, :size], u[:, size + LEAF :]], axis=1) if u.shape[1] > size + LEAF else u[:, :size]
+            for u in updated
+        ]
+    return rests
 
 
 def series(curvatures):
@@ -469,8 +469,7 @@
 
     cross_gram = [c_all[:, :size], c_all[:, size:]]
     normal = [exact(c, c, NT) for c in cross_gram]
-    minus_inverse = invert(normal, leaf, sum_g.share_x)
-    turned = [-exact(m, c) for m, c in zip(minus_inverse, cross_gram)]
+    turned = solve(normal, cross_gram, leaf, sum_g.share_x)
 
     sum_g.finish()
     of_bases = unpack(g_all[:, : 2 * size])

time: 69 us -> 68.7 us (level)
  no operation moved by 1% of the time
where the time goes in v6:
time: 68.7 us; the launch traced here: 68.5 us
  Pallas kernels  63.6 us (93%)
  local copies, waits for them, and re-layouts  4.85 us (7%)
    pallas_call x1, Pallas kernels, body(): pl.pallas_call(functools.partial(kernel, cells, depth * cells, samps), ou...  63.6 us
    unnamed x9, local copies, waits for them, and re-layouts  4.85 us

profile of v6, /device:TPU:8, one launch (start us, length us, event | category | flops | bytes accessed | tf_op | source)
XLA Modules:
  0.0 68.5 jit_solution(11490107012373217791)
XLA Ops:
  0.0 0.0 copy-start
  0.0 1.9 %copy-done = f32[2,2048,192]{1,2,0:T(8,128)S(1)} copy-done((f32[2,2048,192]{1,2,0:T(8,128)S(1)}, f32[2,2048,192]{1,2,0:T(8,128)}, u32[]{:S(2)}) %copy-start) | copy-done | bytes 3145752
  1.9 0.0 copy-start.1
  1.9 0.9 %copy-done.1 = f32[256,192]{0,1:T(8,128)S(1)} copy-done((f32[256,192]{0,1:T(8,128)S(1)}, f32[256,192]{0,1:T(8,128)}, u32[]{:S(2)}) %copy-start.1) | copy-done | bytes 196632
  2.8 0.0 copy-start.2
  2.8 0.7 %copy-done.2 = f32[2048]{0:T(1024)S(1)} copy-done((f32[2048]{0:T(1024)S(1)}, f32[2048]{0:T(1024)}, u32[]{:S(2)}) %copy-start.2) | copy-done | bytes 8216
  3.5 0.0 copy-start.3
  3.5 0.7 copy-done.3
  4.2 63.6 %shard_map.46 = f32[192,256]{1,0:T(8,128)S(1)} custom-call(f32[2,192,2048]{2,1,0:T(8,128)S(1)} %bitcast.4, f32[192,256]{1,0:T(8,128)S(1)} %bitcast.6, f32[1,2048]{1,0:T(1,128)S(1)} %bitcast.7, f32[2]{0:T(128)S(1)} %copy-done.3), custom_call_target="tpu_custom_call" | custom-call | tf_op jit(solution)/shard_map/pallas_call | solution.py:548
  67.8 0.7 copy.6
Async XLA Ops:
  0.0 1.9 %copy-start = (f32[2,2048,192]{1,2,0:T(8,128)S(1)}, f32[2,2048,192]{1,2,0:T(8,128)}, u32[]{:S(2)}) copy-start(f32[2,2048,192]{1,2,0:T(8,128)} %param.4) | copy-start | bytes 9437188
  1.9 0.9 %copy-start.1 = (f32[256,192]{0,1:T(8,128)S(1)}, f32[256,192]{0,1:T(8,128)}, u32[]{:S(2)}) copy-start(f32[256,192]{0,1:T(8,128)} %param.5) | copy-start | bytes 589828
  2.8 0.7 %copy-start.2 = (f32[2048]{0:T(1024)S(1)}, f32[2048]{0:T(1024)}, u32[]{:S(2)}) copy-start(f32[2048]{0:T(1024)} %param.6) | copy-start | bytes 24580
  3.5 0.7 copy-start.3
